TPU v7x, 32 devices: a whole 2x2x4 slice. The times are simulated.
32 devices in a mesh: req: 4 (over x, core), seq: 8 (over z, y).
Axes of the slice: x: 2, y: 2, z: 4, core: 2. Of those that a mesh axis runs over, the one named last changes fastest.
Arguments:
- hidden: bfloat16 [4, 1024, 2048], P('req', 'seq'), may hold values from -6 to 6
- lengths: int32 [4], replicated, may hold values from 1 to 1024, 2560 in all
- slot_request: int32 [4], replicated, may hold values from 0 to 3, each once
- norm_gain: bfloat16 [2048], replicated, may hold values from 0.099609375 to 1.8984375
- in_weight: bfloat16 [2, 2048, 4096], P(None, 'req', 'seq'), may hold values from -0.125 to 0.125
- conv_weight: bfloat16 [4, 4096], P(None, 'seq'), may hold values from -3 to 3
- conv_bias: bfloat16 [4096], P('seq'), may hold values from -0.5 to 0.5
- xproj_weight: bfloat16 [4096, 160], P('seq'), may hold values from -0.09375 to 0.09375
- dt_weight: bfloat16 [128, 4096], P(None, 'seq'), may hold values from -0.5 to 0.5
- dt_bias: bfloat16 [4096], P('seq'), may hold values from -6.91 to -2.25
- a_log: float32 [16, 4096], replicated, may hold values from -2.3 to 1.39
- skip_gain: float32 [4096], replicated, may hold values from 0.5 to 1.5
- out_weight: bfloat16 [4096, 2048], P('seq', 'req'), may hold values from -0.09375 to 0.09375
Outputs:
- mixed: bfloat16 [4, 1024, 2048], P('req', 'seq')
- final_state: float32 [4, 16, 4096], P('req', None, 'seq')
Inputs may be any that keep to these rules, and one draw needn't show every extreme that they name: `lengths`: each slot's length is at least 1, the longest is exactly 1024, and they sum to 2560. `slot_request`: A permutation of the requests.
All inputs are finite; a program needn't handle non-finite values.
Results may differ from a plain program's by a relative error of at most 0.015.
Values may be sent and summed in bfloat16 or wider, within the bound.
A program may use at most 128 MiB of HBM per device.

v0:
```python
import jax
import jax.numpy as jnp
from jax import lax
from jax.sharding import PartitionSpec as P

STATE = 16
RANK = 128


def shifted(block, axis, distance):
    devices = range(lax.axis_size(axis))
    route = [(i - distance, i) for i in devices if i - distance in devices]
    return lax.ppermute(block, axis, route)


def spread(array, axis, root):
    mine = lax.axis_index(axis) == root
    return lax.psum(jnp.where(mine, array, jnp.zeros_like(array)), axis)


def to_blocks(array):
    pieces, length, columns = array.shape
    return jnp.moveaxis(array.reshape(pieces, 16, length // 16, columns), 1, 0)


def from_blocks(array):
    count, pieces, group, columns = array.shape
    return jnp.moveaxis(array, 0, 1).reshape(pieces, count * group, columns)


def piece_scan(rates, values, entry, readout, decay):
    pieces, length, columns = rates.shape
    group = length // 16
    positions = jnp.arange(length, dtype=jnp.int32)
    lower = (positions[None, :] <= positions[:, None]).astype(jnp.float32)
    running = jnp.einsum("rs,psw->prw", lower, rates, precision=lax.Precision.HIGHEST)

    def advance(state, items):
        rate, value, into, outof = items
        outputs = []
        for place in range(group):
            factor = jnp.exp(rate[:, place][:, None, :] * decay[None])
            state = (
                factor * state
                + (rate[:, place] * value[:, place])[:, None, :] * into[:, place][:, :, None]
            )
            outputs.append(jnp.sum(outof[:, place][:, :, None] * state, axis=1))
        return (state, jnp.stack(outputs, axis=1))

    start = jnp.zeros((pieces, decay.shape[0], columns), jnp.float32)
    end_local, local_out = lax.scan(
        advance, start, (to_blocks(rates), to_blocks(values), to_blocks(entry), to_blocks(readout))
    )
    total_decay = jnp.exp(running[:, length - 1][:, None, :] * decay[None])
    return (end_local, from_blocks(local_out), total_decay, running)


def carried_part(running, readout, decay, carry_in):

    def correct(items):
        total, outof = items
        kept = jnp.exp(total[:, :, None, :] * decay[None, None]) * carry_in[:, None]
        return jnp.sum(outof[:, :, :, None] * kept, axis=2)

    return from_blocks(lax.map(correct, (to_blocks(running), to_blocks(readout))))


def per_device(
    hidden,
    lengths,
    slot_request,
    norm_gain,
    in_weight,
    conv_weight,
    conv_bias,
    xproj_weight,
    dt_weight,
    dt_bias,
    a_log,
    skip_gain,
    out_weight,
):
    seq_count = lax.axis_size("seq")
    seq_index = lax.axis_index("seq")
    req_index = lax.axis_index("req")
    rows = hidden.shape[1]
    span = rows * seq_count
    width = in_weight.shape[2]
    taps_count = conv_weight.shape[0]
    state_count = a_log.shape[0]
    total_inner = a_log.shape[1]
    tokens = hidden[0].astype(jnp.float32)
    scale = lax.rsqrt(jnp.mean(tokens * tokens, axis=-1, keepdims=True) + 1e-05)
    normed = (tokens * scale * norm_gain.astype(jnp.float32)).astype(jnp.bfloat16)
    w_in = lax.all_gather(in_weight, "req", axis=1, tiled=True)
    w_flat = jnp.concatenate((w_in[0], w_in[1]), axis=1)
    both = jnp.dot(
        lax.all_gather(normed, "seq", axis=0, tiled=True),
        w_flat,
        preferred_element_type=jnp.float32,
    )
    xin = both[:, :width]
    zgate = both[:, width:].astype(jnp.bfloat16)
    padded = jnp.pad(xin, ((taps_count - 1, 0), (0, 0)))
    taps = conv_weight.astype(jnp.float32)
    convolved = conv_bias.astype(jnp.float32) + jnp.zeros_like(xin)
    for tap in range(taps_count):
        convolved = convolved + taps[tap] * padded[tap : tap + span, :]
    inner = jax.nn.silu(convolved).astype(jnp.bfloat16)
    partial_proj = jnp.dot(inner, xproj_weight, preferred_element_type=jnp.float32)
    length_here = lax.dynamic_index_in_dim(lengths, req_index, 0, keepdims=False)
    summed = lax.psum(partial_proj, "seq")
    live_all = (jnp.arange(span, dtype=jnp.int32) < length_here).astype(jnp.float32)
    rate_low = summed[:, :RANK].astype(jnp.bfloat16)
    delta_ch = (
        jax.nn.softplus(
            jnp.dot(rate_low, dt_weight, preferred_element_type=jnp.float32)
            + dt_bias.astype(jnp.float32)
        )
        * live_all[:, None]
    )
    w_out = lax.all_gather(out_weight, "req", axis=1, tiled=True)
    inner_tok = lax.all_to_all(inner, "seq", split_axis=0, concat_axis=1, tiled=True)
    delta_tok = lax.all_to_all(
        delta_ch.astype(jnp.bfloat16), "seq", split_axis=0, concat_axis=1, tiled=True
    ).astype(delta_ch.dtype)
    own_proj = lax.dynamic_slice_in_dim(summed, seq_index * rows, rows, 0)
    decay = -jnp.exp(a_log)
    inner_f = inner_tok.astype(jnp.float32)
    entry = own_proj[None, :, RANK : RANK + STATE]
    readout = own_proj[None, :, RANK + STATE :]
    end_local, local_out, total_decay, running = piece_scan(
        delta_tok[None], inner_f[None], entry, readout, decay
    )
    zeros_state = jnp.zeros((state_count, total_inner), jnp.float32)

    def relay(turn, incoming):
        return shifted(total_decay[0] * incoming + end_local[0], "seq", 1)

    carry_in = lax.fori_loop(0, seq_count - 1, relay, zeros_state)
    carried = carried_part(running, readout, decay, carry_in[None])
    scanned = ((local_out + carried)[0] + skip_gain * inner_f).astype(jnp.bfloat16)
    last = spread(
        (total_decay[0] * carry_in + end_local[0]).astype(jnp.bfloat16), "seq", seq_count - 1
    ).astype(jnp.float32)
    mine = lax.dynamic_slice_in_dim(last, seq_index * width, width, 1)
    scanned_ch = lax.all_to_all(scanned, "seq", split_axis=1, concat_axis=0, tiled=True)
    gated_ch = (scanned_ch.astype(jnp.float32) * jax.nn.silu(zgate.astype(jnp.float32))).astype(
        jnp.bfloat16
    )
    branch = lax.psum_scatter(
        jnp.dot(gated_ch, w_out, preferred_element_type=jnp.float32).astype(jnp.bfloat16),
        "seq",
        scatter_dimension=0,
        tiled=True,
    ).astype(jnp.float32)
    slot_all = lax.all_gather(mine[None], "req", axis=0, tiled=True)
    picked = (slot_request == req_index).astype(jnp.float32)
    final_state = jnp.sum(picked[:, None, None] * slot_all, axis=0, keepdims=True)
    mixed = (tokens + branch).astype(jnp.bfloat16)[None]
    return (mixed, final_state)


def solution(mesh):
    in_specs = (
        P("req", "seq", None),
        P(),
        P(),
        P(),
        P(None, "req", "seq"),
        P(None, "seq"),
        P("seq"),
        P("seq", None),
        P(None, "seq"),
        P("seq"),
        P(),
        P(),
        P("seq", "req"),
    )
    out_specs = (P("req", "seq", None), P("req", None, "seq"))
    return jax.shard_map(
        per_device, mesh=mesh, in_specs=in_specs, out_specs=out_specs, check_vma=False
    )
```

profile of v0, /device:TPU:0, one launch (start us, length us, event | category | flops | bytes accessed | tf_op | source)
XLA Modules:
  0.0 612.6 jit_solution(8012847031500108282)
XLA Ops:
  9.9 2.0 fusion.42
  12.0 34.8 %all-gather.7.cloned.1.call-done = bf16[2,2048,512]{2,1,0:T(8,128)(2,1)} async-done(((bf16[2,512,512]{2,1,0:T(8,128)(2,1)}), bf16[2,2048,512]{2,1,0:T(8,128)(2,1)}) %all-gather.7.cloned.1.call-update) | async-done | bytes 4194320 | tf_op jit(solution)/shard_map/all_gather | solution.py:95
  46.8 4.5 slice_bitcast_fusion.17
  51.3 71.7 %all-gather.5.cloned.1.call-done = bf16[1024,2048]{1,0:T(8,128)(2,1)} async-done(((bf16[128,2048]{1,0:T(8,128)(2,1)}), bf16[1024,2048]{1,0:T(8,128)(2,1)}) %all-gather.5.cloned.1.call-update) | async-done | bytes 4194320 | tf_op jit(solution)/shard_map/all_gather | solution.py:98
  122.9 7.5 %fusion.24 = f32[1024,1024]{1,0:T(8,128)S(1)} fusion(bf16[1024,2048]{1,0:T(8,128)(2,1)} %all-gather.5.cloned.1.call-done, bf16[2048,512]{1,0:T(8,128)(2,1)} %get-tuple-element.269, bf16[2048,512]{1,0:T(8,128)(2,1)} %get-tuple-element.268), kind=kOutput, calls=%fused_computation.76 | convolution fusion | flops 4303355904 | bytes 12582912 | tf_op jit(solution)/shard_map/dot_general | solution.py:97
  130.8 1.7 copy-done.3
  132.5 2.3 multiply_convert_fusion
  134.8 3.7 all-to-all-start.1
  138.5 2.6 fusion.56
  142.4 83.1 %all-reduce.4.cloned.1.call-done = f32[1024,160]{0,1:T(8,128)} async-done(((f32[1024,160]{0,1:T(8,128)}), f32[1024,160]{0,1:T(8,128)}) %all-reduce.4.cloned.1.call-update) | async-done | bytes 655376 | tf_op jit(solution)/shard_map/psum | solution.py:112
  225.5 2.5 fusion.36
  229.4 3.9 all-to-all-start
  235.0 2.6 copy.45
  237.6 2.8 reshape.994
  240.4 17.4 %all-to-all-done = bf16[8,128,512]{1,2,0:T(8,128)(2,1)S(1)} async-done(((bf16[8,128,512]{1,2,0:T(8,128)(2,1)}), bf16[8,128,512]{1,2,0:T(8,128)(2,1)S(1)}, u32[]{:S(2)}, u32[]{:S(2)}) %all-to-all-start) | async-done | bytes 1048608 | tf_op jit(solution)/shard_map/all_to_all | solution.py:124
  259.6 1.5 bitcast_convert_fusion
  261.0 3.1 copy.44
  264.1 2.8 reshape.993
  267.0 1.5 broadcast.550.clone
  268.5 55.2 %while.35 = (s32[]{:T(128)}, f32[1,16,4096]{2,1,0:T(8,128)S(1)}, f32[16,1,8,4096]{3,2,1,0:T(8,128)}, f32[16,1,8,4096]{3,2,1,0:T(8,128)}, f32[16,4096]{1,0:T(8,12...) while((s32[]{:T(128)}, f32[1,16,4096]{2,1,0:T(8,128)S(1)}, ...), condition=%wide.region_11.12_spmd.clone, body=%wide.region_2.11_spmd.clone.sunk | while | flops 4849667 | bytes 4347896 | solution.py:51
  323.7 63.2 %while.33 = (s32[]{:T(128)}, f32[16,4096]{1,0:T(8,128)S(1)}, f32[1,16,4096]{2,1,0:T(8,128)S(1)}, f32[1,16,4096]{2,1,0:T(8,128)S(1)}, s32[]{:T(128)}) while((s32[]{:T(128)}, f32[16,4096]{1,0:T(8,128)S(1)}, f32[1,16,4096]{2,1,0:T(8,128)S(1)}, f32[1,16,4096]{2,1,0:T(8,128)S(1)}, s32[]{:T(128)}) %tuple.124), condition=%wide.region_13.14_spmd, body=%wide.region_12.13_spmd.sunk | while | flops 131074 | bytes 2097253 | solution.py:140
  323.8 3.2 collective-permute-start
  326.9 4.3 collective-permute-done
  331.3 4.4 collective-permute-start
  335.7 3.9 collective-permute-done
  339.6 4.4 collective-permute-start
  344.0 3.9 collective-permute-done
  347.9 4.4 collective-permute-start
  352.3 4.0 collective-permute-done
  356.3 4.8 collective-permute-start
  361.1 4.6 collective-permute-done
  365.8 5.7 collective-permute-start
  371.5 5.8 collective-permute-done
  377.4 5.6 collective-permute-start
  383.0 3.9 collective-permute-done
  386.9 1.6 broadcast.550
  388.5 35.8 %while.34 = (s32[]{:T(128)}, f32[16,1,8,4096]{3,2,1,0:T(8,128)}, f32[16,1,8,16]{3,2,1,0:T(8,128)S(1)}, f32[16,1,8,4096]{3,2,1,0:T(8,128)}, f32[16,4096]{1,0:T(8,128)S(1)}, /*index=5*/f32[16,4096]{1,0:T(8,128)S(1)}, s32[]{:T(128)}) while((s32[]{:T(128)}, f32[16,1,8,4096]{3,2,1,0:T(8,128)}, f32[16,1,8,16]{3,2,1,0:T(8,128)S(1)}, ...), condition=%wide.region_16.17_spmd, body=%wide.region_14.16_spmd.sunk | while | flops 2064386 | bytes 1312853 | solution.py:65
  424.3 2.5 add.134
  426.8 1.6 copy.54
  428.4 2.2 fusion.34
  430.6 6.6 %all-to-all-start.2 = ((bf16[128,8,512]{2,0,1:T(8,128)(2,1)}), bf16[128,8,512]{2,0,1:T(8,128)(2,1)S(1)}, u32[]{:S(2)}, u32[]{:S(2)}) async-start(bf16[128,8,512]{2,0,1:T(8,128)(2,1)} %fusion.34), calls=%async_computation.2 | async-start | bytes 2097152 | tf_op jit(solution)/shard_map/all_to_all | solution.py:147
  438.3 17.5 %all-to-all-done.2 = bf16[128,8,512]{2,0,1:T(8,128)(2,1)S(1)} async-done(((bf16[128,8,512]{2,0,1:T(8,128)(2,1)}), bf16[128,8,512]{2,0,1:T(8,128)(2,1)S(1)}, u32[]{:S(2)}, u32[]{:S(2)}) %all-to-all-start.2) | async-done | bytes 1048608 | tf_op jit(solution)/shard_map/all_to_all | solution.py:147
  455.8 2.3 fusion.39
  458.2 5.9 convolution_convert_fusion
  464.7 48.4 %all-reduce.6.cloned.1.call-done = bf16[16,4096]{1,0:T(8,128)(2,1)} async-done(((bf16[16,4096]{1,0:T(8,128)(2,1)}), bf16[16,4096]{1,0:T(8,128)(2,1)}) %all-reduce.6.cloned.1.call-update) | async-done | bytes 131088 | tf_op jit(solution)/shard_map/psum | solution.py:18
  513.8 5.4 all-gather
  519.9 83.9 %reduce-scatter.2.cloned.1.call-done = bf16[128,2048]{1,0:T(8,128)(2,1)} async-done(((bf16[1024,2048]{1,0:T(8,128)(2,1)}), bf16[128,2048]{1,0:T(8,128)(2,1)}) %reduce-scatter.2.cloned.1.call-update) | async-done | bytes 524304 | tf_op jit(solution)/shard_map/reduce_scatter | solution.py:151
  603.8 2.0 fusion.44
  (308 shorter events, 102.2 us)
Async XLA Ops:
  7.2 131.3 %copy-start = (bf16[512,160]{0,1:T(8,128)(2,1)S(1)}, bf16[512,160]{0,1:T(8,128)(2,1)}, u32[]{:S(2)}) copy-start(bf16[512,160]{0,1:T(8,128)(2,1)} %param.26) | copy-start | bytes 491524
  7.2 4.8 copy-start.7
  7.2 4.8 copy-start.6
  7.2 39.6 %all-gather.7.cloned.1.call-start = ((), (), s32[]{:S(2)}) async-start(), calls=%async_computation.5 | async-start | bytes 5242880 | tf_op jit(solution)/shard_map/all_gather | solution.py:95
  7.9 115.0 %all-gather.5.cloned.1.call-start = ((), (), s32[]{:S(2)}) async-start(), calls=%async_computation.4 | async-start | bytes 4718592 | tf_op jit(solution)/shard_map/all_gather | solution.py:98
  130.5 2.0 copy-start.3
  134.8 6.4 %copy-start.8 = (bf16[512]{0:T(512)(128)(2,1)S(1)}, bf16[512]{0:T(512)(128)(2,1)}, u32[]{:S(2)}) copy-start(bf16[512]{0:T(512)(128)(2,1)} %param.28) | copy-start | bytes 3076
  134.8 6.4 %copy-start.10 = (s32[4]{0:T(128)S(1)}, s32[4]{0:T(128)}, u32[]{:S(2)}) copy-start(s32[4]{0:T(128)} %param.20) | copy-start | bytes 52
  134.8 90.7 %copy-start.9 = (bf16[128,512]{1,0:T(8,128)(2,1)S(1)}, bf16[128,512]{1,0:T(8,128)(2,1)}, u32[]{:S(2)}) copy-start(bf16[128,512]{1,0:T(8,128)(2,1)} %param.27) | copy-start | bytes 393220
  134.8 94.6 %all-to-all-start.1 = ((bf16[8,128,512]{2,1,0:T(8,128)(2,1)}), bf16[8,128,512]{2,1,0:T(8,128)(2,1)S(1)}, u32[]{:S(2)}, u32[]{:S(2)}) async-start(bf16[8,128,512]{2,1,0:T(8,128)(2,1)} %bitcast.17), calls=%async_computation.1 | async-start | bytes 2097152 | tf_op jit(solution)/shard_map/all_to_all | solution.py:123
  138.5 87.0 %all-reduce.4.cloned.1.call-start = ((), (), s32[]{:S(2)}) async-start(), calls=%async_computation.6 | async-start | bytes 1310720 | tf_op jit(solution)/shard_map/psum | solution.py:112
  228.0 5.8 copy-start.5
  229.4 28.4 %all-to-all-start = ((bf16[8,128,512]{1,2,0:T(8,128)(2,1)}), bf16[8,128,512]{1,2,0:T(8,128)(2,1)S(1)}, u32[]{:S(2)}, u32[]{:S(2)}) async-start(bf16[8,128,512]{1,2,0:T(8,128)(2,1)} %copy.43), calls=%async_computation | async-start | bytes 2097152 | tf_op jit(solution)/shard_map/all_to_all | solution.py:124
  233.2 224.9 %all-gather.9.cloned.1.call-start = ((), (), s32[]{:S(2)}) async-start(), calls=%async_computation.7 | async-start | bytes 2621440 | tf_op jit(solution)/shard_map/all_gather | solution.py:122
  258.2 1.3 copy-start.2
  264.1 2.8 copy-start.4
  323.8 7.5 %collective-permute-start = (f32[16,4096]{1,0:T(8,128)S(1)}, f32[16,4096]{1,0:T(8,128)S(1)}, u32[]{:S(2)}, u32[]{:S(2)}) collective-permute-start(f32[16,4096]{1,0:T(8,128)S(1)} %bitcast_add_fusion.3), channel_id=1, source_target_pairs={{0,1},{1,2},{2,3},{3,4},{4,5},{5,6},{6,7},{8,9},{9,10},{10,11},{11... | collective-permute-start | bytes 786440 | tf_op jit(solution)/shard_map/while/body/eval_jaxpr/ppermute | solution.py:13
  331.3 8.3 %collective-permute-start = (f32[16,4096]{1,0:T(8,128)S(1)}, f32[16,4096]{1,0:T(8,128)S(1)}, u32[]{:S(2)}, u32[]{:S(2)}) collective-permute-start(f32[16,4096]{1,0:T(8,128)S(1)} %bitcast_add_fusion.3), channel_id=1, source_target_pairs={{0,1},{1,2},{2,3},{3,4},{4,5},{5,6},{6,7},{8,9},{9,10},{10,11},{11... | collective-permute-start | bytes 786440 | tf_op jit(solution)/shard_map/while/body/eval_jaxpr/ppermute | solution.py:13
  339.6 8.3 %collective-permute-start = (f32[16,4096]{1,0:T(8,128)S(1)}, f32[16,4096]{1,0:T(8,128)S(1)}, u32[]{:S(2)}, u32[]{:S(2)}) collective-permute-start(f32[16,4096]{1,0:T(8,128)S(1)} %bitcast_add_fusion.3), channel_id=1, source_target_pairs={{0,1},{1,2},{2,3},{3,4},{4,5},{5,6},{6,7},{8,9},{9,10},{10,11},{11... | collective-permute-start | bytes 786440 | tf_op jit(solution)/shard_map/while/body/eval_jaxpr/ppermute | solution.py:13
  347.9 8.4 %collective-permute-start = (f32[16,4096]{1,0:T(8,128)S(1)}, f32[16,4096]{1,0:T(8,128)S(1)}, u32[]{:S(2)}, u32[]{:S(2)}) collective-permute-start(f32[16,4096]{1,0:T(8,128)S(1)} %bitcast_add_fusion.3), channel_id=1, source_target_pairs={{0,1},{1,2},{2,3},{3,4},{4,5},{5,6},{6,7},{8,9},{9,10},{10,11},{11... | collective-permute-start | bytes 786440 | tf_op jit(solution)/shard_map/while/body/eval_jaxpr/ppermute | solution.py:13
  356.3 9.4 %collective-permute-start = (f32[16,4096]{1,0:T(8,128)S(1)}, f32[16,4096]{1,0:T(8,128)S(1)}, u32[]{:S(2)}, u32[]{:S(2)}) collective-permute-start(f32[16,4096]{1,0:T(8,128)S(1)} %bitcast_add_fusion.3), channel_id=1, source_target_pairs={{0,1},{1,2},{2,3},{3,4},{4,5},{5,6},{6,7},{8,9},{9,10},{10,11},{11... | collective-permute-start | bytes 786440 | tf_op jit(solution)/shard_map/while/body/eval_jaxpr/ppermute | solution.py:13
  365.8 11.5 %collective-permute-start = (f32[16,4096]{1,0:T(8,128)S(1)}, f32[16,4096]{1,0:T(8,128)S(1)}, u32[]{:S(2)}, u32[]{:S(2)}) collective-permute-start(f32[16,4096]{1,0:T(8,128)S(1)} %bitcast_add_fusion.3), channel_id=1, source_target_pairs={{0,1},{1,2},{2,3},{3,4},{4,5},{5,6},{6,7},{8,9},{9,10},{10,11},{11... | collective-permute-start | bytes 786440 | tf_op jit(solution)/shard_map/while/body/eval_jaxpr/ppermute | solution.py:13
  377.4 9.5 %collective-permute-start = (f32[16,4096]{1,0:T(8,128)S(1)}, f32[16,4096]{1,0:T(8,128)S(1)}, u32[]{:S(2)}, u32[]{:S(2)}) collective-permute-start(f32[16,4096]{1,0:T(8,128)S(1)} %bitcast_add_fusion.3), channel_id=1, source_target_pairs={{0,1},{1,2},{2,3},{3,4},{4,5},{5,6},{6,7},{8,9},{9,10},{10,11},{11... | collective-permute-start | bytes 786440 | tf_op jit(solution)/shard_map/while/body/eval_jaxpr/ppermute | solution.py:13
  430.6 25.2 %all-to-all-start.2 = ((bf16[128,8,512]{2,0,1:T(8,128)(2,1)}), bf16[128,8,512]{2,0,1:T(8,128)(2,1)S(1)}, u32[]{:S(2)}, u32[]{:S(2)}) async-start(bf16[128,8,512]{2,0,1:T(8,128)(2,1)} %fusion.34), calls=%async_computation.2 | async-start | bytes 2097152 | tf_op jit(solution)/shard_map/all_to_all | solution.py:147
  437.2 75.9 %all-reduce.6.cloned.1.call-start = ((), (), s32[]{:S(2)}) async-start(), calls=%async_computation.9 | async-start | bytes 262144 | tf_op jit(solution)/shard_map/psum | solution.py:18
  438.0 165.7 %reduce-scatter.2.cloned.1.call-start = ((), (), s32[]{:S(2)}) async-start(), calls=%async_computation.8 | async-start | bytes 4718592 | tf_op jit(solution)/shard_map/reduce_scatter | solution.py:151
  464.1 0.7 copy-start.11
  464.1 139.7 %copy-start.1 = (bf16[1,128,2048]{2,1,0:T(8,128)(2,1)S(1)}, bf16[1,128,2048]{2,1,0:T(8,128)(2,1)}, u32[]{:S(2)}) copy-start(bf16[1,128,2048]{2,1,0:T(8,128)(2,1)} %param.19) | copy-start | bytes 1572868
Sparse Core Ops, SparseCore 0:
  9.6 37.1 all-gather.6
  49.5 73.3 all-gather.4
  142.7 82.7 all-reduce.3
  235.4 23.9 all-gather.8
  442.0 70.9 all-reduce.5
  516.6 87.1 reduce-scatter.1
where the time goes:
time: 614 us; the launch traced here: 613 us
  waiting for transfers between devices  388 us (63%)
  local copies, waits for them, and re-layouts  83.6 us (14%)
  other arithmetic  53.3 us (9%)
  starting transfers between devices  47.2 us (8%)
  matrix products  19 us (3%)
  between operations  14.4 us (2%)
    reduce_scatter x1, waiting for transfers between devices, per_device(): lax.psum_scatter(jnp.dot(gated_ch, w_out, preferred_element_type=jnp.floa...  83.9 us
    psum x1, waiting for transfers between devices, per_device(): summed = lax.psum(partial_proj, 'seq')  83.1 us
    all_gather x1, waiting for transfers between devices, per_device(): lax.all_gather(normed, 'seq', axis=0, tiled=True)  71.7 us
    psum x1, waiting for transfers between devices, spread(): return lax.psum(jnp.where(mine, array, jnp.zeros_like(array)), axis)  48.4 us
    all_gather x1, waiting for transfers between devices, per_device(): w_in = lax.all_gather(in_weight, 'req', axis=1, tiled=True)  34.8 us
    ppermute x7, starting transfers between devices, shifted(): return lax.ppermute(block, axis, route)  32.4 us
    ppermute x7, waiting for transfers between devices, shifted(): return lax.ppermute(block, axis, route)  30.3 us
    dynamic_update_slice x32, local copies, waits for them, and re-layouts, piece_scan(): lax.scan(advance, start, (to_blocks(rates), to_blocks(values), to_blocks(...  21.2 us
  transfers between devices with their start and end apart: 16, of which 14 were waited for; matrix products, arithmetic and copies ran while one was open for 23% of the time, Pallas kernels for 0%

commit v1 on v0

v1 whole, which is shorter than its diff:
```python
import functools
import math

import jax
import jax.numpy as jnp
from jax import lax
from jax.experimental import pallas as pl
from jax.experimental.pallas import tpu as pltpu
from jax.sharding import PartitionSpec as P

STATE = 16
RANK = 128
GROUP = 8
VMEM_LIMIT = 48 * 1024 * 1024


def silu(v):
    return v / (1.0 + jnp.exp(-v))


def softplus(v):
    return jnp.maximum(v, 0.0) + jnp.log1p(jnp.exp(-jnp.abs(v)))


def scan_kernel(
    length_ref, low_ref, into_ref, outof_ref, inner_ref, zgate_ref, dtw_ref, dtb_ref, alog_ref, skip_ref,
    gated_ref, final_ref, rate_ref, push_ref, out_ref,
):
    span = inner_ref.shape[0]
    block = 128
    length = length_ref[0]

    @pl.loop(0, span // block)
    def _(i):
        rows = pl.ds(pl.multiple_of(i * block, block), block)
        pre = jnp.dot(low_ref[rows, :], dtw_ref[...], preferred_element_type=jnp.float32)
        rate = softplus(pre + dtb_ref[...].astype(jnp.float32))
        place = lax.broadcasted_iota(jnp.int32, rate.shape, 0) + i * block
        rate = jnp.where(place < length, rate, 0.0)
        rate_ref[rows, :] = rate
        push_ref[rows, :] = rate * inner_ref[rows, :].astype(jnp.float32)

    decay = -jnp.exp(alog_ref[...]) * math.log2(math.e)
    state_shape = decay.shape

    def advance(i, state):
        start = pl.multiple_of(i * GROUP, GROUP)
        tile = pl.ds(pl.multiple_of((i // (128 // GROUP)) * 128, 128), 128)
        shift = lax.rem(128 - lax.rem(i, 128 // GROUP) * GROUP, 128)
        into = pltpu.roll(into_ref[:, tile], shift, 1)
        outof = pltpu.roll(outof_ref[:, tile], shift, 1)
        rows = []
        for j in range(GROUP):
            rate = rate_ref[pl.ds(start + j, 1), :]
            push = push_ref[pl.ds(start + j, 1), :]
            factor = jnp.exp2(jnp.broadcast_to(rate, state_shape) * decay)
            state = factor * state + jnp.broadcast_to(push, state_shape) * into[:, j : j + 1]
            rows.append(jnp.sum(state * outof[:, j : j + 1], axis=0, keepdims=True))
        out_ref[pl.ds(start, GROUP), :] = jnp.concatenate(rows, axis=0)
        return state

    final_ref[...] = lax.fori_loop(0, span // GROUP, advance, jnp.zeros(state_shape, jnp.float32))

    @pl.loop(0, span // block)
    def _(i):
        rows = pl.ds(pl.multiple_of(i * block, block), block)
        scanned = out_ref[rows, :] + skip_ref[...] * inner_ref[rows, :].astype(jnp.float32)
        scanned = scanned.astype(jnp.bfloat16).astype(jnp.float32)
        gated_ref[rows, :] = (scanned * silu(zgate_ref[rows, :].astype(jnp.float32))).astype(jnp.bfloat16)


def scan_call(length, low, into, outof, inner, zgate, dtw, dtb, alog, skip):
    span, width = inner.shape
    vmem = pl.BlockSpec(memory_space=pltpu.VMEM)
    return pl.pallas_call(
        scan_kernel,
        out_shape=(
            jax.ShapeDtypeStruct((span, width), jnp.bfloat16),
            jax.ShapeDtypeStruct((STATE, width), jnp.float32),
        ),
        in_specs=[pl.BlockSpec(memory_space=pltpu.SMEM)] + [vmem] * 9,
        out_specs=(vmem, vmem),
        scratch_shapes=[pltpu.VMEM((span, width), jnp.float32)] * 3,
        compiler_params=pltpu.CompilerParams(vmem_limit_bytes=VMEM_LIMIT),
        cost_estimate=pl.CostEstimate(
            flops=span * width * STATE * 7, bytes_accessed=span * width * 8, transcendentals=span * width * STATE
        ),
        name="scan",
    )(length, low, into, outof, inner, zgate, dtw, dtb, alog, skip)


def per_device(
    hidden,
    lengths,
    slot_request,
    norm_gain,
    in_weight,
    conv_weight,
    conv_bias,
    xproj_weight,
    dt_weight,
    dt_bias,
    a_log,
    skip_gain,
    out_weight,
):
    seq_count = lax.axis_size("seq")
    seq_index = lax.axis_index("seq")
    req_index = lax.axis_index("req")
    rows = hidden.shape[1]
    span = rows * seq_count
    width = in_weight.shape[2]
    taps_count = conv_weight.shape[0]
    tokens = hidden[0].astype(jnp.float32)
    scale = lax.rsqrt(jnp.mean(tokens * tokens, axis=-1, keepdims=True) + 1e-05)
    normed = (tokens * scale * norm_gain.astype(jnp.float32)).astype(jnp.bfloat16)
    w_in = lax.all_gather(in_weight, "req", axis=1, tiled=True)
    w_flat = jnp.concatenate((w_in[0], w_in[1]), axis=1)
    both = jnp.dot(
        lax.all_gather(normed, "seq", axis=0, tiled=True),
        w_flat,
        preferred_element_type=jnp.float32,
    )
    xin = both[:, :width]
    zgate = both[:, width:].astype(jnp.bfloat16)
    padded = jnp.pad(xin, ((taps_count - 1, 0), (0, 0)))
    taps = conv_weight.astype(jnp.float32)
    convolved = conv_bias.astype(jnp.float32) + jnp.zeros_like(xin)
    for tap in range(taps_count):
        convolved = convolved + taps[tap] * padded[tap : tap + span, :]
    inner = jax.nn.silu(convolved).astype(jnp.bfloat16)
    partial_proj = jnp.dot(inner, xproj_weight, preferred_element_type=jnp.float32)
    summed = lax.psum(partial_proj, "seq")
    w_out = lax.all_gather(out_weight, "req", axis=1, tiled=True)
    length_here = lax.dynamic_slice_in_dim(lengths, req_index, 1, 0)
    low = summed[:, :RANK].astype(jnp.bfloat16)
    into = summed[:, RANK : RANK + STATE].T
    outof = summed[:, RANK + STATE :].T
    alog = lax.dynamic_slice_in_dim(a_log, seq_index * width, width, 1)
    skip = lax.dynamic_slice_in_dim(skip_gain, seq_index * width, width, 0)[None]
    gated_ch, mine = scan_call(
        length_here, low, into, outof, inner, zgate, dt_weight, dt_bias[None], alog, skip
    )
    branch = lax.psum_scatter(
        jnp.dot(gated_ch, w_out, preferred_element_type=jnp.float32).astype(jnp.bfloat16),
        "seq",
        scatter_dimension=0,
        tiled=True,
    ).astype(jnp.float32)
    slot_all = lax.all_gather(mine[None], "req", axis=0, tiled=True)
    picked = (slot_request == req_index).astype(jnp.float32)
    final_state = jnp.sum(picked[:, None, None] * slot_all, axis=0, keepdims=True)
    mixed = (tokens + branch).astype(jnp.bfloat16)[None]
    return (mixed, final_state)


def solution(mesh):
    in_specs = (
        P("req", "seq", None),
        P(),
        P(),
        P(),
        P(None, "req", "seq"),
        P(None, "seq"),
        P("seq"),
        P("seq", None),
        P(None, "seq"),
        P("seq"),
        P(),
        P(),
        P("seq", "req"),
    )
    out_specs = (P("req", "seq", None), P("req", None, "seq"))
    return jax.shard_map(
        per_device, mesh=mesh, in_specs=in_specs, out_specs=out_specs, check_vma=False
    )
```

time: 614 us -> 344 us (0.56)
  waiting for transfers between devices: 388 us -> 257 us
  local copies, waits for them, and re-layouts: 83.6 us -> 12.7 us
  starting transfers between devices: 47.2 us -> 0.2 us
  other arithmetic: 53.3 us -> 7.95 us
  Pallas kernels: 0 us -> 31.5 us
    psum x1 -> x0, waiting for transfers between devices: 48.4 us -> none  [spread(): return lax.psum(jnp.where(mine, array, jnp.zeros_like(array)), axis)]
    all_to_all x3 -> x0, waiting for transfers between devices: 34.9 us -> none  [the longest x1 17.5 us: per_device(): lax.all_to_all(scanned, 'seq', split_axis=1, concat_axis=0, tiled=True)]
    ppermute x7 -> x0, starting transfers between devices: 32.4 us -> none  [shifted(): return lax.ppermute(block, axis, route)]
    pallas_call x0 -> x1, Pallas kernels: none -> 31.5 us  [scan_call(): pl.pallas_call(scan_kernel, out_shape=(jax.ShapeDtypeStruct((span, width)...]
    ppermute x7 -> x0, waiting for transfers between devices: 30.3 us -> none  [shifted(): return lax.ppermute(block, axis, route)]
    reduce_sum x64 -> x0, other arithmetic: 29.9 us -> none  [the longest x48 19.8 us: advance(): outputs.append(jnp.sum(outof[:, place][:, :, None] * state, axis=1))]
    dynamic_update_slice x32 -> x0, local copies, waits for them, and re-layouts: 21.2 us -> none  [piece_scan(): lax.scan(advance, start, (to_blocks(rates), to_blocks(values), to_blocks(...]
    squeeze x32 -> x0, local copies, waits for them, and re-layouts: 15.9 us -> none  [piece_scan(): lax.scan(advance, start, (to_blocks(rates), to_blocks(values), to_blocks(...]
  transfers between devices with their start and end apart: 16 -> 5, of which waited for: 14 -> 4; matrix products, arithmetic and copies ran while one was open for 23% -> 4% of each run, Pallas kernels for 0% -> 9%
where the time goes in v1:
time: 344 us; the launch traced here: 343 us
  waiting for transfers between devices  257 us (75%)
  Pallas kernels  31.5 us (9%)
  matrix products  14.5 us (4%)
  between operations  14 us (4%)
  local copies, waits for them, and re-layouts  12.7 us (4%)
  other arithmetic  7.95 us (2%)
  blocking collectives  5.41 us (2%)
    reduce_scatter x1, waiting for transfers between devices, per_device(): lax.psum_scatter(jnp.dot(gated_ch, w_out, preferred_element_type=jnp.floa...  80.6 us
    all_gather x1, waiting for transfers between devices, per_device(): lax.all_gather(normed, 'seq', axis=0, tiled=True)  72.3 us
    psum x1, waiting for transfers between devices, per_device(): summed = lax.psum(partial_proj, 'seq')  68 us
    all_gather x1, waiting for transfers between devices, per_device(): w_in = lax.all_gather(in_weight, 'req', axis=1, tiled=True)  34.7 us
    pallas_call x1, Pallas kernels, scan_call(): pl.pallas_call(scan_kernel, out_shape=(jax.ShapeDtypeStruct((span, width)...  31.5 us
    dot_general x1, matrix products, per_device(): jnp.dot(lax.all_gather(normed, 'seq', axis=0, tiled=True), w_flat, prefer...  6.9 us
  transfers between devices with their start and end apart: 5, of which 4 were waited for; matrix products, arithmetic and copies ran while one was open for 4% of the time, Pallas kernels for 9%

profile of v1, /device:TPU:0, one launch (start us, length us, event | category | flops | bytes accessed | tf_op | source)
XLA Modules:
  0.0 343.1 jit_solution(13804815922945541256)
XLA Ops:
  7.2 0.0 copy-start
  7.2 0.0 copy-start.7
  7.2 0.0 copy-start.6
  7.2 0.0 all-gather.7.cloned.1.call-start
  7.2 0.7 all-gather.7.cloned.1.call-update
  7.9 0.0 all-gather.5.cloned.1.call-start
  8.0 0.7 convert_element_type.41
  8.7 1.2 fusion.6
  9.9 2.0 fusion.8
  11.9 0.0 all-gather.5.cloned.1.call-update
  12.0 0.0 all-reduce.3.cloned.1.call-start
  12.0 0.0 copy-done.7
  12.0 0.0 copy-done.6
  12.1 34.7 %all-gather.7.cloned.1.call-done = bf16[2,2048,512]{2,1,0:T(8,128)(2,1)} async-done(((bf16[2,512,512]{2,1,0:T(8,128)(2,1)}), bf16[2,2048,512]{2,1,0:T(8,128)(2,1)}) %all-gather.7.cloned.1.call-update) | async-done | bytes 4194320 | tf_op jit(solution)/shard_map/all_gather | solution.py:117
  46.8 3.9 %slice_bitcast_fusion.1 = (bf16[2048,512]{1,0:T(8,128)(2,1)S(1)}, bf16[2048,512]{1,0:T(8,128)(2,1)}) fusion(bf16[2,2048,512]{2,1,0:T(8,128)(2,1)} %all-gather.7.cloned.1.call-done), kind=kLoop, calls=%fused_computation.7 | loop fusion | bytes 8388608 | tf_op jit(solution)/shard_map/squeeze | solution.py:118
  50.7 72.3 %all-gather.5.cloned.1.call-done = bf16[1024,2048]{1,0:T(8,128)(2,1)} async-done(((bf16[128,2048]{1,0:T(8,128)(2,1)}), bf16[1024,2048]{1,0:T(8,128)(2,1)}) %all-gather.5.cloned.1.call-update) | async-done | bytes 4194320 | tf_op jit(solution)/shard_map/all_gather | solution.py:120
  122.9 6.9 %fusion = f32[1024,1024]{1,0:T(8,128)S(1)} fusion(bf16[1024,2048]{1,0:T(8,128)(2,1)} %all-gather.5.cloned.1.call-done, bf16[2048,512]{1,0:T(8,128)(2,1)} %get-tuple-element.7, bf16[2048,512]{1,0:T(8,128)(2,1)S(1)} %get-tuple-element.6), kind=kOutput, calls=%fused_computation | convolution fusion | flops 4303355904 | bytes 12582912 | tf_op jit(solution)/shard_map/dot_general | solution.py:119
  129.9 0.0 copy-start.4
  129.9 0.2 slice.62
  130.1 1.7 copy-done.4
  131.8 1.3 multiply_convert_fusion.inner_ref
  133.2 0.0 copy-done.5
  133.2 0.0 copy-start.8
  133.2 0.0 copy-start.9
  133.2 1.3 fusion.13
  134.5 0.0 all-reduce.3.cloned.1.call-update
  134.5 0.0 copy-start.1
  134.6 0.0 all-gather.9.cloned.1.call-start
  134.6 0.5 all-gather.9.cloned.1.call-update
  135.1 0.0 reduce-scatter.2.cloned.1.call-start
  135.2 0.0 copy-done.8
  135.2 0.6 dynamic_slice.9.length_ref
  135.8 0.8 dynamic_slice.11
  136.6 1.7 slice.85.zgate_ref
  138.3 68.0 %all-reduce.3.cloned.1.call-done = f32[1024,160]{0,1:T(8,128)} async-done(((f32[1024,160]{0,1:T(8,128)}), f32[1024,160]{0,1:T(8,128)}) %all-reduce.3.cloned.1.call-update) | async-done | bytes 655376 | tf_op jit(solution)/shard_map/psum | solution.py:133
  206.3 1.1 slice.86
  207.4 0.2 copy.15.low_ref
  207.6 0.9 slice_bitcast_fusion.2
  208.4 0.0 copy-done.1
  208.5 31.5 %scan.1 = (bf16[1024,512]{1,0:T(8,128)(2,1)S(1)}, f32[16,512]{1,0:T(8,128)S(1)}) custom-call(s32[1]{0:T(128)} %dynamic_slice.9.length_ref, bf16[1024,128]{1,0:T(8,128)(2,1)S(1)} %copy.15.low_ref, f32[16,1024]{1,0:T(8,128)S(1)} %get-tuple-element.9.into_ref, f32[16,1024]{1,0:T(8,128)S(1)} %get-tuple-element.8.outof_ref, ...), custom_call_target="tpu_custom_call" | custom-call | flops 58720256 | bytes 4194304 | tf_op jit(solution)/shard_map/scan/pallas_call | solution.py:75
  240.0 1.0 copy-done.2
  241.0 6.2 %convolution_convert_fusion = bf16[1024,2048]{1,0:T(8,128)(2,1)} fusion(bf16[1024,512]{1,0:T(8,128)(2,1)} %copy-done.2, bf16[512,2048]{1,0:T(8,128)(2,1)} %all-gather.9.cloned.1.call-done), kind=kOutput, calls=%fused_computation.4 | convolution fusion | flops 2149580800 | bytes 7340032 | tf_op jit(solution)/shard_map/dot_general | solution.py:145
  247.2 0.0 reduce-scatter.2.cloned.1.call-update
  247.2 0.6 copy-done.10
  247.9 5.4 %all-gather = f32[64,512]{1,0:T(8,128)S(1)} all-gather(f32[16,512]{1,0:T(8,128)S(1)} %get-tuple-element.5), channel_id=2, replica_groups=mesh['req'=4,'seq'=8] {'req'}, dimensions={0}, use_global_device_ids=true | all-gather | bytes 163840 | tf_op jit(solution)/shard_map/all_gather | solution.py:150
  253.3 0.7 multiply_reduce_fusion
  254.0 80.6 %reduce-scatter.2.cloned.1.call-done = bf16[128,2048]{1,0:T(8,128)(2,1)} async-done(((bf16[1024,2048]{1,0:T(8,128)(2,1)}), bf16[128,2048]{1,0:T(8,128)(2,1)}) %reduce-scatter.2.cloned.1.call-update) | async-done | bytes 524304 | tf_op jit(solution)/shard_map/reduce_scatter | solution.py:144
  334.6 2.0 fusion.10
  (14 shorter events, 0.0 us)
Async XLA Ops:
  7.2 129.4 %copy-start = (f32[16,4096]{1,0:T(8,128)S(1)}, f32[16,4096]{1,0:T(8,128)}, u32[]{:S(2)}) copy-start(f32[16,4096]{1,0:T(8,128)} %param.23) | copy-start | bytes 786436
  7.2 4.8 %copy-start.7 = (bf16[512]{0:T(512)(128)(2,1)S(1)}, bf16[512]{0:T(512)(128)(2,1)}, u32[]{:S(2)}) copy-start(bf16[512]{0:T(512)(128)(2,1)} %param.19) | copy-start | bytes 3076
  7.2 4.8 %copy-start.6 = (bf16[4,512]{1,0:T(4,128)(2,1)S(1)}, bf16[4,512]{1,0:T(4,128)(2,1)}, u32[]{:S(2)}) copy-start(bf16[4,512]{1,0:T(4,128)(2,1)} %param.18) | copy-start | bytes 12292
  7.2 39.6 %all-gather.7.cloned.1.call-start = ((), (), s32[]{:S(2)}) async-start(), calls=%async_computation.2 | async-start | bytes 5242880 | tf_op jit(solution)/shard_map/all_gather | solution.py:117
  7.9 115.0 %all-gather.5.cloned.1.call-start = ((), (), s32[]{:S(2)}) async-start(), calls=%async_computation.1 | async-start | bytes 4718592 | tf_op jit(solution)/shard_map/all_gather | solution.py:120
  12.0 194.3 %all-reduce.3.cloned.1.call-start = ((), (), s32[]{:S(2)}) async-start(), calls=%async_computation.3 | async-start | bytes 1310720 | tf_op jit(solution)/shard_map/psum | solution.py:133
  129.9 2.0 copy-start.4
  131.8 1.3 copy-start.5
  133.2 2.0 copy-start.8
  133.2 2.0 copy-start.9
  134.5 73.9 %copy-start.1 = (bf16[128,512]{1,0:T(8,128)(2,1)S(1)}, bf16[128,512]{1,0:T(8,128)(2,1)}, u32[]{:S(2)}) copy-start(bf16[128,512]{1,0:T(8,128)(2,1)} %dtw_ref.1) | copy-start | bytes 393220
  134.6 106.4 %all-gather.9.cloned.1.call-start = ((), (), s32[]{:S(2)}) async-start(), calls=%async_computation.4 | async-start | bytes 2621440 | tf_op jit(solution)/shard_map/all_gather | solution.py:134
  135.1 199.4 %reduce-scatter.2.cloned.1.call-start = ((), (), s32[]{:S(2)}) async-start(), calls=%async_computation.5 | async-start | bytes 4718592 | tf_op jit(solution)/shard_map/reduce_scatter | solution.py:144
  240.0 1.0 copy-start.2
  247.2 0.7 copy-start.10
  247.2 87.4 %copy-start.3 = (bf16[1,128,2048]{2,1,0:T(8,128)(2,1)S(1)}, bf16[1,128,2048]{2,1,0:T(8,128)(2,1)}, u32[]{:S(2)}) copy-start(bf16[1,128,2048]{2,1,0:T(8,128)(2,1)} %param.13) | copy-start | bytes 1572868
Sparse Core Ops, SparseCore 0:
  9.6 37.1 all-gather.6
  49.5 73.3 all-gather.4
  134.7 71.5 all-reduce.2
  207.8 21.8 all-gather.8
  247.4 87.1 reduce-scatter.1

commit v2 on v1

--- a/solution.py
+++ b/solution.py
@@ -87,6 +87,273 @@
         ),
         name="scan",
     )(length, low, into, outof, inner, zgate, dtw, dtb, alog, skip)
+
+
+def ring_place(index, count):
+    half = count // 2
+    y, z = index % 2, index // 2
+    return y * (2 * half - 1) + z * (1 - 2 * y)
+
+
+def ring_index(place, count):
+    half = count // 2
+    y = place // half
+    return 2 * (place * (1 - 2 * y) + y * (2 * half - 1)) + y
+
+
+def greet(peers):
+    barrier = pltpu.get_barrier_semaphore()
+    for peer in peers:
+        pl.semaphore_signal(barrier, inc=1, device_id=peer, device_id_type=pl.DeviceIdType.MESH)
+    pl.semaphore_wait(barrier, len(peers))
+
+
+def remote(src, dst, send, recv, peer):
+    return pltpu.make_async_remote_copy(
+        src_ref=src, dst_ref=dst, send_sem=send, recv_sem=recv, device_id=peer,
+        device_id_type=pl.DeviceIdType.MESH,
+    )
+
+
+def gather_kernel(
+    n, m, normed_ref, win_ref, wout_ref, act_ref, wg_ref, og_ref,
+    ring_send, ring_recv, x_send, x_recv, c_send, c_recv, local_sem,
+):
+    rows = normed_ref.shape[0]
+    half = rows // 2
+    depth = win_ref.shape[1]
+    req, seq = lax.axis_index("req"), lax.axis_index("seq")
+    place = ring_place(seq, n)
+    right = (req, ring_index((place + 1) % n, n))
+    left = (req, ring_index((place + n - 1) % n, n))
+    chips = m // 2
+    chip, core = req // 2, req % 2
+    ahead = (((chip + 1) % chips) * 2 + core, seq)
+    behind = (((chip + chips - 1) % chips) * 2 + core, seq)
+    mate = (chip * 2 + 1 - core, seq)
+    greet([left, right, mate, ahead] + ([behind] if chips > 2 else []))
+
+    def win_at(owner):
+        return wg_ref.at[:, pl.ds(pl.multiple_of(owner * depth, depth), depth), :]
+
+    def wout_at(owner):
+        return og_ref.at[:, pl.ds(pl.multiple_of(owner * depth, depth), depth)]
+
+    pending = []
+    crossing = []
+    for which, (src, at) in enumerate(((win_ref, win_at), (wout_ref, wout_at))):
+        crossing.append(remote(src, at(req), x_send.at[which, 0], x_recv.at[which, 0], ahead))
+        crossing[-1].start()
+        own = remote(src, at(req), c_send.at[which, 0], c_recv.at[which, 0], mate)
+        own.start()
+        pending.append(own)
+    locals_ = [
+        pltpu.make_async_copy(normed_ref, act_ref.at[seq], local_sem.at[0]),
+        pltpu.make_async_copy(win_ref, win_at(req), local_sem.at[1]),
+        pltpu.make_async_copy(wout_ref, wout_at(req), local_sem.at[2]),
+    ]
+    for copy in locals_:
+        copy.start()
+
+    ring = []
+    for step in range(n - 1):
+        pair = []
+        for way in range(2):
+            part = pl.ds(way * half, half)
+            turn = place + (n - step if way == 0 else step)
+            owner = ring_index(turn % n, n)
+            src = normed_ref.at[part] if step == 0 else act_ref.at[owner, part]
+            copy = remote(
+                src, act_ref.at[owner, part], ring_send.at[way, step], ring_recv.at[way, step],
+                right if way == 0 else left,
+            )
+            copy.start()
+            pair.append(copy)
+        if step == n - 2:
+            for hop in range(1, chips):
+                owner = ((chip + chips - hop) % chips) * 2 + core
+                coming = crossing
+                crossing = []
+                for which, at in enumerate((win_at, wout_at)):
+                    coming[which].wait()
+                    block = at(owner)
+                    passed = remote(block, block, c_send.at[which, hop], c_recv.at[which, hop], mate)
+                    passed.start()
+                    pending.append(passed)
+                    if hop < chips - 1:
+                        crossing.append(remote(block, block, x_send.at[which, hop], x_recv.at[which, hop], ahead))
+                        crossing[-1].start()
+        for copy in pair:
+            copy.wait_recv()
+        ring += pair
+    for copy in ring:
+        copy.wait_send()
+    for copy in pending:
+        copy.wait()
+    for copy in locals_:
+        copy.wait()
+
+
+def gather_call(n, m, normed, win, wout):
+    rows, model = normed.shape
+    _, depth, width = win.shape
+    anywhere = pl.BlockSpec(memory_space=pl.ANY)
+    dma = pltpu.SemaphoreType.DMA
+    return pl.pallas_call(
+        functools.partial(gather_kernel, n, m),
+        out_shape=(
+            jax.ShapeDtypeStruct((n, rows, model), jnp.bfloat16),
+            jax.ShapeDtypeStruct((2, depth * m, width), jnp.bfloat16),
+            jax.ShapeDtypeStruct((width, depth * m), jnp.bfloat16),
+        ),
+        in_specs=[anywhere] * 3,
+        out_specs=(anywhere,) * 3,
+        scratch_shapes=[
+            dma((2, n - 1)), dma((2, n - 1)), dma((2, m // 2 - 1)), dma((2, m // 2 - 1)),
+            dma((2, m // 2)), dma((2, m // 2)), dma((3,)),
+        ],
+        compiler_params=pltpu.CompilerParams(
+            collective_id=0, has_side_effects=True, vmem_limit_bytes=VMEM_LIMIT
+        ),
+        name="gather",
+    )(normed, win, wout)
+
+
+def total_kernel(n, part_ref, sum_ref, send_buf, recv_buf, own_buf, send, recv, send2, recv2):
+    req, seq = lax.axis_index("req"), lax.axis_index("seq")
+    peers = [(req, (seq + d) % n) for d in range(1, n)]
+    greet(peers)
+    send_buf[...] = part_ref[...].astype(jnp.bfloat16)
+    first = []
+    for d in range(1, n):
+        copy = remote(
+            send_buf.at[(seq + d) % n], recv_buf.at[d - 1], send.at[d - 1], recv.at[d - 1], peers[d - 1]
+        )
+        copy.start()
+        first.append(copy)
+    total = part_ref[seq]
+    for d in range(1, n):
+        first[d - 1].wait_recv()
+        total = total + recv_buf[d - 1].astype(jnp.float32)
+    own_buf[...] = total.astype(jnp.bfloat16)
+    sum_ref[seq] = own_buf[...]
+    second = []
+    for d in range(1, n):
+        copy = remote(own_buf, sum_ref.at[seq], send2.at[d - 1], recv2.at[d - 1], peers[d - 1])
+        copy.start()
+        second.append(copy)
+    for copy in second:
+        copy.wait()
+    for copy in first:
+        copy.wait_send()
+
+
+def total_call(n, part):
+    vmem = pl.BlockSpec(memory_space=pltpu.VMEM)
+    dma = pltpu.SemaphoreType.DMA
+    _, rows, columns = part.shape
+    return pl.pallas_call(
+        functools.partial(total_kernel, n),
+        out_shape=jax.ShapeDtypeStruct(part.shape, jnp.bfloat16),
+        in_specs=[vmem],
+        out_specs=vmem,
+        scratch_shapes=[
+            pltpu.VMEM((n, rows, columns), jnp.bfloat16),
+            pltpu.VMEM((n - 1, rows, columns), jnp.bfloat16),
+            pltpu.VMEM((rows, columns), jnp.bfloat16),
+        ] + [dma((n - 1,))] * 4,
+        compiler_params=pltpu.CompilerParams(
+            collective_id=1, has_side_effects=True, vmem_limit_bytes=VMEM_LIMIT
+        ),
+        name="total",
+    )(part)
+
+
+def output_kernel(
+    n, m, gated_ref, wout_ref, hidden_ref, state_ref, mixed_ref, slots_ref,
+    send_buf, recv_buf, acc_ref, send, recv, state_send, state_recv,
+):
+    rows, model = hidden_ref.shape
+    half = model // 2
+    req, seq = lax.axis_index("req"), lax.axis_index("seq")
+    place = ring_place(seq, n)
+    right = (req, ring_index((place + 1) % n, n))
+    left = (req, ring_index((place + n - 1) % n, n))
+    peers = [((req + d) % m, seq) for d in range(1, m)]
+    greet([left, right] + peers)
+    states = []
+    for d in range(1, m):
+        copy = remote(state_ref, slots_ref.at[req], state_send.at[d - 1], state_recv.at[d - 1], peers[d - 1])
+        copy.start()
+        states.append(copy)
+    slots_ref[req] = state_ref[...]
+
+    def hop(way, step):
+        return remote(
+            send_buf.at[way, step], recv_buf.at[way, step], send.at[way, step], recv.at[way, step],
+            right if way == 0 else left,
+        )
+
+    def product(way, step):
+        turn = place + (2 * n - 1 - step if way == 0 else 1 + step)
+        owner = ring_index(turn % n, n)
+        block = gated_ref[pl.ds(pl.multiple_of(owner * rows, rows), rows), :]
+        acc_ref[way] = jnp.dot(
+            block, wout_ref[:, way * half : (way + 1) * half], preferred_element_type=jnp.float32
+        )
+
+    for way in range(2):
+        product(way, 0)
+        send_buf[way, 0] = acc_ref[way].astype(jnp.bfloat16)
+        hop(way, 0).start()
+
+    def middle(step, carry):
+        for way in range(2):
+            product(way, step)
+        for way in range(2):
+            hop(way, step - 1).wait_recv()
+            send_buf[way, step] = (acc_ref[way] + recv_buf[way, step - 1].astype(jnp.float32)).astype(jnp.bfloat16)
+            hop(way, step).start()
+        return carry
+
+    lax.fori_loop(1, n - 1, middle, 0)
+    for way in range(2):
+        product(way, n - 1)
+    for way in range(2):
+        hop(way, n - 2).wait_recv()
+        columns = slice(way * half, (way + 1) * half)
+        branch = acc_ref[way] + recv_buf[way, n - 2].astype(jnp.float32)
+        mixed_ref[:, columns] = (hidden_ref[:, columns].astype(jnp.float32) + branch).astype(jnp.bfloat16)
+    for step in range(n - 1):
+        for way in range(2):
+            hop(way, step).wait_send()
+    for copy in states:
+        copy.wait()
+
+
+def output_call(n, m, gated, wout, hidden, state):
+    rows, model = hidden.shape
+    vmem = pl.BlockSpec(memory_space=pltpu.VMEM)
+    dma = pltpu.SemaphoreType.DMA
+    return pl.pallas_call(
+        functools.partial(output_kernel, n, m),
+        out_shape=(
+            jax.ShapeDtypeStruct((rows, model), jnp.bfloat16),
+            jax.ShapeDtypeStruct((m,) + state.shape, jnp.float32),
+        ),
+        in_specs=[vmem] * 4,
+        out_specs=(vmem, vmem),
+        scratch_shapes=[
+            pltpu.VMEM((2, n - 1, rows, model // 2), jnp.bfloat16),
+            pltpu.VMEM((2, n - 1, rows, model // 2), jnp.bfloat16),
+            pltpu.VMEM((2, rows, model // 2), jnp.float32),
+            dma((2, n - 1)), dma((2, n - 1)), dma((m - 1,)), dma((m - 1,)),
+        ],
+        compiler_params=pltpu.CompilerParams(
+            collective_id=2, has_side_effects=True, vmem_limit_bytes=VMEM_LIMIT
+        ),
+        name="output",
+    )(gated, wout, hidden, state)
 
 
 def per_device(
@@ -114,15 +381,11 @@
     tokens = hidden[0].astype(jnp.float32)
     scale = lax.rsqrt(jnp.mean(tokens * tokens, axis=-1, keepdims=True) + 1e-05)
     normed = (tokens * scale * norm_gain.astype(jnp.float32)).astype(jnp.bfloat16)
-    w_in = lax.all_gather(in_weight, "req", axis=1, tiled=True)
-    w_flat = jnp.concatenate((w_in[0], w_in[1]), axis=1)
-    both = jnp.dot(
-        lax.all_gather(normed, "seq", axis=0, tiled=True),
-        w_flat,
-        preferred_element_type=jnp.float32,
-    )
-    xin = both[:, :width]
-    zgate = both[:, width:].astype(jnp.bfloat16)
+    req_count = lax.axis_size("req")
+    act, w_in, w_out = gather_call(seq_count, req_count, normed, in_weight, out_weight)
+    act = act.reshape(span, -1)
+    xin = jnp.dot(act, w_in[0], preferred_element_type=jnp.float32)
+    zgate = jnp.dot(act, w_in[1], preferred_element_type=jnp.float32).astype(jnp.bfloat16)
     padded = jnp.pad(xin, ((taps_count - 1, 0), (0, 0)))
     taps = conv_weight.astype(jnp.float32)
     convolved = conv_bias.astype(jnp.float32) + jnp.zeros_like(xin)
@@ -130,28 +393,20 @@
         convolved = convolved + taps[tap] * padded[tap : tap + span, :]
     inner = jax.nn.silu(convolved).astype(jnp.bfloat16)
     partial_proj = jnp.dot(inner, xproj_weight, preferred_element_type=jnp.float32)
-    summed = lax.psum(partial_proj, "seq")
-    w_out = lax.all_gather(out_weight, "req", axis=1, tiled=True)
+    summed = total_call(seq_count, partial_proj.reshape(seq_count, rows, -1)).reshape(span, -1)
     length_here = lax.dynamic_slice_in_dim(lengths, req_index, 1, 0)
-    low = summed[:, :RANK].astype(jnp.bfloat16)
-    into = summed[:, RANK : RANK + STATE].T
-    outof = summed[:, RANK + STATE :].T
+    low = summed[:, :RANK]
+    into = summed[:, RANK : RANK + STATE].astype(jnp.float32).T
+    outof = summed[:, RANK + STATE :].astype(jnp.float32).T
     alog = lax.dynamic_slice_in_dim(a_log, seq_index * width, width, 1)
     skip = lax.dynamic_slice_in_dim(skip_gain, seq_index * width, width, 0)[None]
     gated_ch, mine = scan_call(
         length_here, low, into, outof, inner, zgate, dt_weight, dt_bias[None], alog, skip
     )
-    branch = lax.psum_scatter(
-        jnp.dot(gated_ch, w_out, preferred_element_type=jnp.float32).astype(jnp.bfloat16),
-        "seq",
-        scatter_dimension=0,
-        tiled=True,
-    ).astype(jnp.float32)
-    slot_all = lax.all_gather(mine[None], "req", axis=0, tiled=True)
+    mixed, slot_all = output_call(seq_count, req_count, gated_ch, w_out, hidden[0], mine)
     picked = (slot_request == req_index).astype(jnp.float32)
     final_state = jnp.sum(picked[:, None, None] * slot_all, axis=0, keepdims=True)
-    mixed = (tokens + branch).astype(jnp.bfloat16)[None]
-    return (mixed, final_state)
+    return (mixed[None], final_state)
 
 
 def solution(mesh):

time: 344 us -> 185 us (0.54)
  waiting for transfers between devices: 257 us -> 0 us
  Pallas kernels: 31.5 us -> 163 us
  between operations: 14 us -> 0.92 us
  local copies, waits for them, and re-layouts: 12.7 us -> 3.65 us
  blocking collectives: 5.41 us -> 0 us
    pallas_call x0 -> x3, Pallas kernels: none -> 131 us  [the longest x1 54.3 us: output_call(): pl.pallas_call(functools.partial(output_kernel, n, m), out_shape=(jax.Sha...]
    all_gather x3 -> x0, waiting for transfers between devices: 107 us -> none  [the longest x1 72.3 us: per_device(): lax.all_gather(normed, 'seq', axis=0, tiled=True)]
    reduce_scatter x1 -> x0, waiting for transfers between devices: 80.6 us -> none  [per_device(): lax.psum_scatter(jnp.dot(gated_ch, w_out, preferred_element_type=jnp.floa...]
    psum x1 -> x0, waiting for transfers between devices: 68 us -> none  [per_device(): summed = lax.psum(partial_proj, 'seq')]
    all_gather x1 -> x0, blocking collectives: 5.41 us -> none  [per_device(): slot_all = lax.all_gather(mine[None], 'req', axis=0, tiled=True)]
    squeeze x1 -> x0, local copies, waits for them, and re-layouts: 3.88 us -> none  [per_device(): w_flat = jnp.concatenate((w_in[0], w_in[1]), axis=1)]
  transfers between devices with their start and end apart: 5 -> 0, of which waited for: 4 -> 0; matrix products, arithmetic and copies ran while one was open for 4% -> 0% of each run, Pallas kernels for 9% -> 0%
where the time goes in v2:
time: 185 us; the launch traced here: 184 us
  Pallas kernels  163 us (88%)
  matrix products  11.6 us (6%)
  other arithmetic  5.32 us (3%)
  local copies, waits for them, and re-layouts  3.65 us (2%)
    pallas_call x1, Pallas kernels, output_call(): pl.pallas_call(functools.partial(output_kernel, n, m), out_shape=(jax.Sha...  54.3 us
    pallas_call x1, Pallas kernels, gather_call(): pl.pallas_call(functools.partial(gather_kernel, n, m), out_shape=(jax.Sha...  52.2 us
    pallas_call x1, Pallas kernels, scan_call(): pl.pallas_call(scan_kernel, out_shape=(jax.ShapeDtypeStruct((span, width)...  31.7 us
    pallas_call x1, Pallas kernels, total_call(): pl.pallas_call(functools.partial(total_kernel, n), out_shape=jax.ShapeDty...  24.7 us
    dot_general x1, matrix products, per_device(): xin = jnp.dot(act, w_in[0], preferred_element_type=jnp.float32)  5.94 us
    dot_general x1, matrix products, per_device(): jnp.dot(act, w_in[1], preferred_element_type=jnp.float32)  5.22 us

profile of v2, /device:TPU:0, one launch (start us, length us, event | category | flops | bytes accessed | tf_op | source)
XLA Modules:
  0.0 184.4 jit_solution(16672236469961618446)
XLA Ops:
  0.6 0.0 copy-start
  0.6 0.0 copy-start.4
  0.7 0.8 convert_element_type.31
  1.4 1.2 fusion.11
  2.7 1.2 fusion.13.normed_ref
  3.9 0.0 copy-done.4
  3.9 0.0 copy-start.5
  3.9 1.0 copy-done.5
  5.0 52.2 %gather.1 = (bf16[8,128,2048]{2,1,0:T(8,128)(2,1)}, bf16[2,2048,512]{2,1,0:T(8,128)(2,1)}, bf16[512,2048]{1,0:T(8,128)(2,1)S(1)}) custom-call(bf16[128,2048]{1,0:T(8,128)(2,1)S(1)} %fusion.13.normed_ref, bf16[2,512,512]{2,1,0:T(8,128)(2,1)S(1)} %copy-done.4, bf16[512,512]{1,0:T(8,128)(2,1)S(1)} %copy-done.5), custom_call_target="tpu_custom_call" | custom-call | tf_op jit(solution)/shard_map/gather/pallas_call | solution.py:202
  57.2 0.0 copy-start.2
  57.2 0.0 copy-start.8
  57.2 0.0 copy-start.9
  57.2 5.9 %fusion.2 = f32[1024,512]{1,0:T(8,128)S(1)} fusion(bf16[1024,2048]{1,0:T(8,128)(2,1)} %bitcast.40, bf16[2,2048,512]{2,1,0:T(8,128)(2,1)} %get-tuple-element.10), kind=kOutput, calls=%fused_computation.2 | convolution fusion | flops 2147483648 | bytes 8388608 | tf_op jit(solution)/shard_map/dot_general | solution.py:387
  63.2 0.0 copy-done.2
  63.2 0.0 copy-done.8
  63.2 0.0 copy-start.7
  63.2 0.0 copy-done.9
  63.2 1.3 multiply_convert_fusion.inner_ref
  64.6 0.0 copy-done.7
  64.6 0.4 fusion.16
  65.0 0.0 copy-start.11
  65.1 24.7 %total.1 = bf16[8,128,160]{2,1,0:T(8,128)(2,1)S(1)} custom-call(f32[8,128,160]{2,1,0:T(8,128)S(1)} %bitcast.30), custom_call_target="tpu_custom_call" | custom-call | tf_op jit(solution)/shard_map/total/pallas_call | solution.py:255
  89.7 0.1 fusion.14
  89.9 0.1 copy.21
  90.0 0.1 copy.22
  90.2 0.0 copy-done.11
  90.2 0.6 dynamic_slice.9.length_ref
  90.8 0.0 copy-done
  90.8 0.8 dynamic_slice.11
  91.5 0.0 copy-start.10
  91.5 0.0 copy-start.6
  91.5 5.2 %fusion.8.zgate_ref = bf16[1024,512]{1,0:T(8,128)(2,1)S(1)} fusion(bf16[1024,2048]{1,0:T(8,128)(2,1)} %bitcast.41, bf16[2,2048,512]{2,1,0:T(8,128)(2,1)} %get-tuple-element.10), kind=kOutput, calls=%fused_computation.10 | convolution fusion | flops 2148007936 | bytes 7340032 | tf_op jit(solution)/shard_map/dot_general | solution.py:388
  96.8 0.0 copy-done.10
  96.8 0.0 copy-done.6
  96.8 0.0 copy-start.1
  96.8 0.0 copy-start.3
  96.8 31.7 %scan.1 = (bf16[1024,512]{1,0:T(8,128)(2,1)S(1)}, f32[16,512]{1,0:T(8,128)S(1)}) custom-call(s32[1]{0:T(128)} %dynamic_slice.9.length_ref, bf16[1024,128]{1,0:T(8,128)(2,1)S(1)} %slice.53.low_ref, f32[16,1024]{1,0:T(8,128)S(1)} %get-tuple-element.23.into_ref, f32[16,1024]{1,0:T(8,128)S(1)} %get-tuple-element.22.outof_ref, ...), custom_call_target="tpu_custom_call" | custom-call | flops 58720256 | bytes 4194304 | tf_op jit(solution)/shard_map/scan/pallas_call | solution.py:75
  128.5 0.0 copy-start.12
  128.5 0.0 copy-done.1
  128.5 0.0 copy-done.3
  128.5 54.3 %output.1 = (bf16[128,2048]{1,0:T(8,128)(2,1)S(1)}, f32[4,16,512]{2,1,0:T(8,128)S(1)}) custom-call(bf16[1024,512]{1,0:T(8,128)(2,1)S(1)} %get-tuple-element.11.gated_ref, bf16[512,2048]{1,0:T(8,128)(2,1)S(1)} %copy-done.3, bf16[128,2048]{1,0:T(8,128)(2,1)S(1)} %bitcast.29, f32[16,512]{1,0:T(8,128)S(1)} %get-tuple-element.13.state_ref), custom_call_target="tpu_custom_call" | custom-call | tf_op jit(solution)/shard_map/output/pallas_call | solution.py:338
  182.9 0.0 copy-done.12
  182.9 0.7 multiply_reduce_fusion
  183.6 0.8 copy.24
  (8 shorter events, 0.1 us)
Async XLA Ops:
  0.6 90.1 %copy-start = (f32[16,4096]{1,0:T(8,128)S(1)}, f32[16,4096]{1,0:T(8,128)}, u32[]{:S(2)}) copy-start(f32[16,4096]{1,0:T(8,128)} %param.23) | copy-start | bytes 786436
  0.6 3.3 %copy-start.4 = (bf16[2,512,512]{2,1,0:T(8,128)(2,1)S(1)}, bf16[2,512,512]{2,1,0:T(8,128)(2,1)}, u32[]{:S(2)}) copy-start(bf16[2,512,512]{2,1,0:T(8,128)(2,1)} %win_ref.1) | copy-start | bytes 3145732
  3.9 1.0 copy-start.5
  57.2 6.0 %copy-start.2 = (bf16[512,2048]{1,0:T(8,128)(2,1)}, bf16[512,2048]{1,0:T(8,128)(2,1)S(1)}, u32[]{:S(2)}) copy-start(bf16[512,2048]{1,0:T(8,128)(2,1)S(1)} %get-tuple-element.12.wout_ref) | copy-start | bytes 6291460
  57.2 6.0 %copy-start.8 = (bf16[4,512]{1,0:T(4,128)(2,1)S(1)}, bf16[4,512]{1,0:T(4,128)(2,1)}, u32[]{:S(2)}) copy-start(bf16[4,512]{1,0:T(4,128)(2,1)} %param.18) | copy-start | bytes 12292
  57.2 6.0 %copy-start.9 = (bf16[512]{0:T(512)(128)(2,1)S(1)}, bf16[512]{0:T(512)(128)(2,1)}, u32[]{:S(2)}) copy-start(bf16[512]{0:T(512)(128)(2,1)} %param.19) | copy-start | bytes 3076
  63.2 1.4 copy-start.7
  65.0 25.1 %copy-start.11 = (s32[4]{0:T(128)S(1)}, s32[4]{0:T(128)}, u32[]{:S(2)}) copy-start(s32[4]{0:T(128)} %param.14) | copy-start | bytes 52
  91.5 5.2 %copy-start.10 = (bf16[512]{0:T(512)(128)(2,1)S(1)}, bf16[512]{0:T(512)(128)(2,1)}, u32[]{:S(2)}) copy-start(bf16[512]{0:T(512)(128)(2,1)} %param.22) | copy-start | bytes 3076
  91.5 5.2 %copy-start.6 = (bf16[128,512]{1,0:T(8,128)(2,1)S(1)}, bf16[128,512]{1,0:T(8,128)(2,1)}, u32[]{:S(2)}) copy-start(bf16[128,512]{1,0:T(8,128)(2,1)} %dtw_ref.1) | copy-start | bytes 393220
  96.8 31.7 %copy-start.1 = (bf16[1,128,2048]{2,1,0:T(8,128)(2,1)S(1)}, bf16[1,128,2048]{2,1,0:T(8,128)(2,1)}, u32[]{:S(2)}) copy-start(bf16[1,128,2048]{2,1,0:T(8,128)(2,1)} %param.13) | copy-start | bytes 1572868
  96.8 31.7 %copy-start.3 = (bf16[512,2048]{1,0:T(8,128)(2,1)S(1)}, bf16[512,2048]{1,0:T(8,128)(2,1)}, u32[]{:S(2)}) copy-start(bf16[512,2048]{1,0:T(8,128)(2,1)} %copy-done.2) | copy-start | bytes 6291460
  128.5 54.4 %copy-start.12 = (s32[4]{0:T(128)S(1)}, s32[4]{0:T(128)}, u32[]{:S(2)}) copy-start(s32[4]{0:T(128)} %param.15) | copy-start | bytes 52

commit v3 on v2

--- a/solution.py
+++ b/solution.py
@@ -23,53 +23,43 @@
 
 
 def scan_kernel(
-    length_ref, low_ref, into_ref, outof_ref, inner_ref, zgate_ref, dtw_ref, dtb_ref, alog_ref, skip_ref,
+    length_ref, sums_ref, inner_ref, zgate_ref, dtw_ref, dtb_ref, alog_ref, skip_ref,
     gated_ref, final_ref, rate_ref, push_ref, out_ref,
 ):
-    span = inner_ref.shape[0]
-    block = 128
+    blocks, _, rows = sums_ref.shape
     length = length_ref[0]
-
-    @pl.loop(0, span // block)
-    def _(i):
-        rows = pl.ds(pl.multiple_of(i * block, block), block)
-        pre = jnp.dot(low_ref[rows, :], dtw_ref[...], preferred_element_type=jnp.float32)
-        rate = softplus(pre + dtb_ref[...].astype(jnp.float32))
-        place = lax.broadcasted_iota(jnp.int32, rate.shape, 0) + i * block
-        rate = jnp.where(place < length, rate, 0.0)
-        rate_ref[rows, :] = rate
-        push_ref[rows, :] = rate * inner_ref[rows, :].astype(jnp.float32)
-
     decay = -jnp.exp(alog_ref[...]) * math.log2(math.e)
     state_shape = decay.shape
 
     def advance(i, state):
-        start = pl.multiple_of(i * GROUP, GROUP)
-        tile = pl.ds(pl.multiple_of((i // (128 // GROUP)) * 128, 128), 128)
-        shift = lax.rem(128 - lax.rem(i, 128 // GROUP) * GROUP, 128)
-        into = pltpu.roll(into_ref[:, tile], shift, 1)
-        outof = pltpu.roll(outof_ref[:, tile], shift, 1)
-        rows = []
-        for j in range(GROUP):
-            rate = rate_ref[pl.ds(start + j, 1), :]
-            push = push_ref[pl.ds(start + j, 1), :]
-            factor = jnp.exp2(jnp.broadcast_to(rate, state_shape) * decay)
-            state = factor * state + jnp.broadcast_to(push, state_shape) * into[:, j : j + 1]
-            rows.append(jnp.sum(state * outof[:, j : j + 1], axis=0, keepdims=True))
-        out_ref[pl.ds(start, GROUP), :] = jnp.concatenate(rows, axis=0)
+        here = pl.ds(pl.multiple_of(i * rows, rows), rows)
+        low = sums_ref[i, :RANK, :].astype(jnp.float32).T.astype(jnp.bfloat16)
+        pre = jnp.dot(low, dtw_ref[...], preferred_element_type=jnp.float32)
+        rates = softplus(pre + dtb_ref[...].astype(jnp.float32))
+        place = lax.broadcasted_iota(jnp.int32, rates.shape, 0) + i * rows
+        rates = jnp.where(place < length, rates, 0.0)
+        rate_ref[...] = rates
+        push_ref[...] = rates * inner_ref[here, :].astype(jnp.float32)
+        into = sums_ref[i, RANK : RANK + STATE, :].astype(jnp.float32)
+        outof = sums_ref[i, RANK + STATE :, :].astype(jnp.float32)
+        for start in range(0, rows, GROUP):
+            lines = []
+            for t in range(start, start + GROUP):
+                rate = rate_ref[t : t + 1, :]
+                push = push_ref[t : t + 1, :]
+                factor = jnp.exp2(jnp.broadcast_to(rate, state_shape) * decay)
+                state = factor * state + jnp.broadcast_to(push, state_shape) * into[:, t : t + 1]
+                lines.append(jnp.sum(state * outof[:, t : t + 1], axis=0, keepdims=True))
+            out_ref[start : start + GROUP, :] = jnp.concatenate(lines, axis=0)
+        scanned = out_ref[...] + skip_ref[...] * inner_ref[here, :].astype(jnp.float32)
+        scanned = scanned.astype(jnp.bfloat16).astype(jnp.float32)
+        gated_ref[here, :] = (scanned * silu(zgate_ref[here, :].astype(jnp.float32))).astype(jnp.bfloat16)
         return state
 
-    final_ref[...] = lax.fori_loop(0, span // GROUP, advance, jnp.zeros(state_shape, jnp.float32))
-
-    @pl.loop(0, span // block)
-    def _(i):
-        rows = pl.ds(pl.multiple_of(i * block, block), block)
-        scanned = out_ref[rows, :] + skip_ref[...] * inner_ref[rows, :].astype(jnp.float32)
-        scanned = scanned.astype(jnp.bfloat16).astype(jnp.float32)
-        gated_ref[rows, :] = (scanned * silu(zgate_ref[rows, :].astype(jnp.float32))).astype(jnp.bfloat16)
-
-
-def scan_call(length, low, into, outof, inner, zgate, dtw, dtb, alog, skip):
+    final_ref[...] = lax.fori_loop(0, blocks, advance, jnp.zeros(state_shape, jnp.float32))
+
+
+def scan_call(length, sums, inner, zgate, dtw, dtb, alog, skip):
     span, width = inner.shape
     vmem = pl.BlockSpec(memory_space=pltpu.VMEM)
     return pl.pallas_call(
@@ -78,15 +68,15 @@
             jax.ShapeDtypeStruct((span, width), jnp.bfloat16),
             jax.ShapeDtypeStruct((STATE, width), jnp.float32),
         ),
-        in_specs=[pl.BlockSpec(memory_space=pltpu.SMEM)] + [vmem] * 9,
+        in_specs=[pl.BlockSpec(memory_space=pltpu.SMEM)] + [vmem] * 7,
         out_specs=(vmem, vmem),
-        scratch_shapes=[pltpu.VMEM((span, width), jnp.float32)] * 3,
+        scratch_shapes=[pltpu.VMEM((sums.shape[2], width), jnp.float32)] * 3,
         compiler_params=pltpu.CompilerParams(vmem_limit_bytes=VMEM_LIMIT),
         cost_estimate=pl.CostEstimate(
             flops=span * width * STATE * 7, bytes_accessed=span * width * 8, transcendentals=span * width * STATE
         ),
         name="scan",
-    )(length, low, into, outof, inner, zgate, dtw, dtb, alog, skip)
+    )(length, sums, inner, zgate, dtw, dtb, alog, skip)
 
 
 def ring_place(index, count):
@@ -219,54 +209,60 @@
     )(normed, win, wout)
 
 
-def total_kernel(n, part_ref, sum_ref, send_buf, recv_buf, own_buf, send, recv, send2, recv2):
+def total_kernel(n, inner_ref, weight_ref, sum_ref, send_buf, recv_buf, own_buf, send, recv, send2, recv2):
     req, seq = lax.axis_index("req"), lax.axis_index("seq")
+    rows = inner_ref.shape[0] // n
     peers = [(req, (seq + d) % n) for d in range(1, n)]
+
+    def partial(owner):
+        block = inner_ref[pl.ds(pl.multiple_of(owner * rows, rows), rows), :]
+        return lax.dot_general(
+            weight_ref[...], block, (((1,), (1,)), ((), ())), preferred_element_type=jnp.float32
+        )
+
     greet(peers)
-    send_buf[...] = part_ref[...].astype(jnp.bfloat16)
     first = []
     for d in range(1, n):
-        copy = remote(
-            send_buf.at[(seq + d) % n], recv_buf.at[d - 1], send.at[d - 1], recv.at[d - 1], peers[d - 1]
-        )
+        send_buf[d - 1] = partial((seq + d) % n).astype(jnp.bfloat16)
+        copy = remote(send_buf.at[d - 1], recv_buf.at[d - 1], send.at[d - 1], recv.at[d - 1], peers[d - 1])
         copy.start()
         first.append(copy)
-    total = part_ref[seq]
+    total = partial(seq)
     for d in range(1, n):
         first[d - 1].wait_recv()
         total = total + recv_buf[d - 1].astype(jnp.float32)
     own_buf[...] = total.astype(jnp.bfloat16)
-    sum_ref[seq] = own_buf[...]
     second = []
     for d in range(1, n):
         copy = remote(own_buf, sum_ref.at[seq], send2.at[d - 1], recv2.at[d - 1], peers[d - 1])
         copy.start()
         second.append(copy)
+    sum_ref[seq] = own_buf[...]
     for copy in second:
         copy.wait()
     for copy in first:
         copy.wait_send()
 
 
-def total_call(n, part):
+def total_call(n, inner, weight):
     vmem = pl.BlockSpec(memory_space=pltpu.VMEM)
     dma = pltpu.SemaphoreType.DMA
-    _, rows, columns = part.shape
+    columns, rows = weight.shape[0], inner.shape[0] // n
     return pl.pallas_call(
         functools.partial(total_kernel, n),
-        out_shape=jax.ShapeDtypeStruct(part.shape, jnp.bfloat16),
-        in_specs=[vmem],
+        out_shape=jax.ShapeDtypeStruct((n, columns, rows), jnp.bfloat16),
+        in_specs=[vmem, vmem],
         out_specs=vmem,
         scratch_shapes=[
-            pltpu.VMEM((n, rows, columns), jnp.bfloat16),
-            pltpu.VMEM((n - 1, rows, columns), jnp.bfloat16),
-            pltpu.VMEM((rows, columns), jnp.bfloat16),
+            pltpu.VMEM((n - 1, columns, rows), jnp.bfloat16),
+            pltpu.VMEM((n - 1, columns, rows), jnp.bfloat16),
+            pltpu.VMEM((columns, rows), jnp.bfloat16),
         ] + [dma((n - 1,))] * 4,
         compiler_params=pltpu.CompilerParams(
             collective_id=1, has_side_effects=True, vmem_limit_bytes=VMEM_LIMIT
         ),
         name="total",
-    )(part)
+    )(inner, weight)
 
 
 def output_kernel(
@@ -392,16 +388,12 @@
     for tap in range(taps_count):
         convolved = convolved + taps[tap] * padded[tap : tap + span, :]
     inner = jax.nn.silu(convolved).astype(jnp.bfloat16)
-    partial_proj = jnp.dot(inner, xproj_weight, preferred_element_type=jnp.float32)
-    summed = total_call(seq_count, partial_proj.reshape(seq_count, rows, -1)).reshape(span, -1)
+    sums = total_call(seq_count, inner, xproj_weight.T)
     length_here = lax.dynamic_slice_in_dim(lengths, req_index, 1, 0)
-    low = summed[:, :RANK]
-    into = summed[:, RANK : RANK + STATE].astype(jnp.float32).T
-    outof = summed[:, RANK + STATE :].astype(jnp.float32).T
     alog = lax.dynamic_slice_in_dim(a_log, seq_index * width, width, 1)
     skip = lax.dynamic_slice_in_dim(skip_gain, seq_index * width, width, 0)[None]
     gated_ch, mine = scan_call(
-        length_here, low, into, outof, inner, zgate, dt_weight, dt_bias[None], alog, skip
+        length_here, sums, inner, zgate, dt_weight, dt_bias[None], alog, skip
     )
     mixed, slot_all = output_call(seq_count, req_count, gated_ch, w_out, hidden[0], mine)
     picked = (slot_request == req_index).astype(jnp.float32)

time: 185 us -> 162 us (0.88)
  Pallas kernels: 163 us -> 140 us
    pallas_call x1, Pallas kernels: 31.7 us -> 16.4 us  [scan_call(): pl.pallas_call(scan_kernel, out_shape=(jax.ShapeDtypeStruct((span, width)...]
    pallas_call x1, Pallas kernels: 24.7 us -> 17.5 us  [total_call(): pl.pallas_call(functools.partial(total_kernel, n), out_shape=jax.ShapeDty...]
where the time goes in v3:
time: 162 us; the launch traced here: 161 us
  Pallas kernels  140 us (86%)
  matrix products  10.4 us (6%)
  other arithmetic  5.3 us (3%)
  local copies, waits for them, and re-layouts  3.97 us (2%)
    pallas_call x1, Pallas kernels, output_call(): pl.pallas_call(functools.partial(output_kernel, n, m), out_shape=(jax.Sha...  53.9 us
    pallas_call x1, Pallas kernels, gather_call(): pl.pallas_call(functools.partial(gather_kernel, n, m), out_shape=(jax.Sha...  52.2 us
    pallas_call x1, Pallas kernels, total_call(): pl.pallas_call(functools.partial(total_kernel, n), out_shape=jax.ShapeDty...  17.5 us
    pallas_call x1, Pallas kernels, scan_call(): pl.pallas_call(scan_kernel, out_shape=(jax.ShapeDtypeStruct((span, width)...  16.4 us
    dot_general x1, matrix products, per_device(): jnp.dot(act, w_in[1], preferred_element_type=jnp.float32)  5.22 us
    dot_general x1, matrix products, per_device(): xin = jnp.dot(act, w_in[0], preferred_element_type=jnp.float32)  5.19 us

profile of v3, /device:TPU:0, one launch (start us, length us, event | category | flops | bytes accessed | tf_op | source)
XLA Modules:
  0.0 160.5 jit_solution(13725610809044683342)
XLA Ops:
  0.6 0.0 copy-start
  0.6 0.0 copy-start.2
  0.7 0.8 convert_element_type.29
  1.4 1.2 fusion.11
  2.7 1.2 fusion.13.normed_ref
  3.9 0.0 copy-done.2
  3.9 0.0 copy-start.3
  3.9 1.0 copy-done.3
  5.0 52.2 %gather.1 = (bf16[8,128,2048]{2,1,0:T(8,128)(2,1)}, bf16[2,2048,512]{2,1,0:T(8,128)(2,1)}, bf16[512,2048]{1,0:T(8,128)(2,1)S(1)}) custom-call(bf16[128,2048]{1,0:T(8,128)(2,1)S(1)} %fusion.13.normed_ref, bf16[2,512,512]{2,1,0:T(8,128)(2,1)S(1)} %copy-done.2, bf16[512,512]{1,0:T(8,128)(2,1)S(1)} %copy-done.3), custom_call_target="tpu_custom_call" | custom-call | tf_op jit(solution)/shard_map/gather/pallas_call | solution.py:192
  57.2 0.0 copy-start.8
  57.2 0.0 copy-start.9
  57.2 5.2 %fusion.2 = f32[1024,512]{1,0:T(8,128)S(1)} fusion(bf16[1024,2048]{1,0:T(8,128)(2,1)} %bitcast.31, bf16[2,2048,512]{2,1,0:T(8,128)(2,1)} %get-tuple-element.10), kind=kOutput, calls=%fused_computation.2 | convolution fusion | flops 2147483648 | bytes 8388608 | tf_op jit(solution)/shard_map/dot_general | solution.py:383
  62.4 0.0 copy-done.8
  62.4 0.0 copy-start.6
  62.5 0.0 copy-done.9
  62.5 0.0 copy-start.11
  62.5 1.3 multiply_convert_fusion.inner_ref
  63.8 0.0 copy-done.6
  63.8 17.5 %total.1.sums_ref = bf16[8,160,128]{2,1,0:T(8,128)(2,1)S(1)} custom-call(bf16[1024,512]{1,0:T(8,128)(2,1)S(1)} %multiply_convert_fusion.inner_ref, bf16[160,512]{1,0:T(8,128)(2,1)S(1)} %bitcast.24), custom_call_target="tpu_custom_call" | custom-call | tf_op jit(solution)/shard_map/total/pallas_call | solution.py:251
  81.3 0.0 copy-start.4
  81.3 0.7 copy-done.4
  82.0 0.0 copy-done.11
  82.0 0.6 dynamic_slice.9.length_ref
  82.6 0.0 copy-done
  82.6 0.8 dynamic_slice.11
  83.4 0.0 copy-start.10
  83.4 0.0 copy-start.5
  83.4 0.0 copy-start.7
  83.4 5.2 %fusion.8.zgate_ref = bf16[1024,512]{1,0:T(8,128)(2,1)S(1)} fusion(bf16[1024,2048]{1,0:T(8,128)(2,1)} %bitcast.32, bf16[2,2048,512]{2,1,0:T(8,128)(2,1)} %get-tuple-element.10), kind=kOutput, calls=%fused_computation.10 | convolution fusion | flops 2148007936 | bytes 7340032 | tf_op jit(solution)/shard_map/dot_general | solution.py:384
  88.6 0.0 copy-done.10
  88.6 0.0 copy-done.5
  88.6 0.0 copy-done.7
  88.7 0.0 copy-start.1
  88.7 16.4 %scan.1 = (bf16[1024,512]{1,0:T(8,128)(2,1)S(1)}, f32[16,512]{1,0:T(8,128)S(1)}) custom-call(s32[1]{0:T(128)} %dynamic_slice.9.length_ref, bf16[8,160,128]{2,1,0:T(8,128)(2,1)S(1)} %copy-done.5, bf16[1024,512]{1,0:T(8,128)(2,1)S(1)} %multiply_convert_fusion.inner_ref, bf16[1024,512]{1,0:T(8,128)(2,1)S(1)} %fusion.8.zgate_ref, ...), custom_call_target="tpu_custom_call" | custom-call | flops 58720256 | bytes 4194304 | tf_op jit(solution)/shard_map/scan/pallas_call | solution.py:65
  105.1 0.0 copy-start.12
  105.1 0.0 copy-done.1
  105.1 53.9 %output.1 = (bf16[128,2048]{1,0:T(8,128)(2,1)S(1)}, f32[4,16,512]{2,1,0:T(8,128)S(1)}) custom-call(bf16[1024,512]{1,0:T(8,128)(2,1)S(1)} %get-tuple-element.11.gated_ref, bf16[512,2048]{1,0:T(8,128)(2,1)S(1)} %get-tuple-element.12.wout_ref, bf16[128,2048]{1,0:T(8,128)(2,1)S(1)} %bitcast.22, f32[16,512]{1,0:T(8,128)S(1)} %get-tuple-element.13.state_ref), custom_call_target="tpu_custom_call" | custom-call | tf_op jit(solution)/shard_map/output/pallas_call | solution.py:334
  159.0 0.0 copy-done.12
  159.0 0.7 multiply_reduce_fusion
  159.7 0.8 copy.16
  (6 shorter events, 0.0 us)
Async XLA Ops:
  0.6 82.0 %copy-start = (f32[16,4096]{1,0:T(8,128)S(1)}, f32[16,4096]{1,0:T(8,128)}, u32[]{:S(2)}) copy-start(f32[16,4096]{1,0:T(8,128)} %param.23) | copy-start | bytes 786436
  0.6 3.3 %copy-start.2 = (bf16[2,512,512]{2,1,0:T(8,128)(2,1)S(1)}, bf16[2,512,512]{2,1,0:T(8,128)(2,1)}, u32[]{:S(2)}) copy-start(bf16[2,512,512]{2,1,0:T(8,128)(2,1)} %win_ref.1) | copy-start | bytes 3145732
  3.9 1.0 copy-start.3
  57.2 5.2 %copy-start.8 = (bf16[4,512]{1,0:T(4,128)(2,1)S(1)}, bf16[4,512]{1,0:T(4,128)(2,1)}, u32[]{:S(2)}) copy-start(bf16[4,512]{1,0:T(4,128)(2,1)} %param.18) | copy-start | bytes 12292
  57.2 5.2 %copy-start.9 = (bf16[512]{0:T(512)(128)(2,1)S(1)}, bf16[512]{0:T(512)(128)(2,1)}, u32[]{:S(2)}) copy-start(bf16[512]{0:T(512)(128)(2,1)} %param.19) | copy-start | bytes 3076
  62.4 1.4 copy-start.6
  62.5 19.6 %copy-start.11 = (s32[4]{0:T(128)S(1)}, s32[4]{0:T(128)}, u32[]{:S(2)}) copy-start(s32[4]{0:T(128)} %param.14) | copy-start | bytes 52
  81.3 0.7 copy-start.4
  83.4 5.2 %copy-start.10 = (bf16[512]{0:T(512)(128)(2,1)S(1)}, bf16[512]{0:T(512)(128)(2,1)}, u32[]{:S(2)}) copy-start(bf16[512]{0:T(512)(128)(2,1)} %param.22) | copy-start | bytes 3076
  83.4 5.3 %copy-start.5 = (bf16[8,160,128]{2,1,0:T(8,128)(2,1)S(1)}, bf16[8,160,128]{2,1,0:T(8,128)(2,1)}, u32[]{:S(2)}) copy-start(bf16[8,160,128]{2,1,0:T(8,128)(2,1)} %copy-done.4) | copy-start | bytes 983044
  83.4 5.3 %copy-start.7 = (bf16[128,512]{1,0:T(8,128)(2,1)S(1)}, bf16[128,512]{1,0:T(8,128)(2,1)}, u32[]{:S(2)}) copy-start(bf16[128,512]{1,0:T(8,128)(2,1)} %dtw_ref.1) | copy-start | bytes 393220
  88.7 16.4 %copy-start.1 = (bf16[1,128,2048]{2,1,0:T(8,128)(2,1)S(1)}, bf16[1,128,2048]{2,1,0:T(8,128)(2,1)}, u32[]{:S(2)}) copy-start(bf16[1,128,2048]{2,1,0:T(8,128)(2,1)} %param.13) | copy-start | bytes 1572868
  105.1 53.9 %copy-start.12 = (s32[4]{0:T(128)S(1)}, s32[4]{0:T(128)}, u32[]{:S(2)}) copy-start(s32[4]{0:T(128)} %param.15) | copy-start | bytes 52

commit v4 on v3

--- a/solution.py
+++ b/solution.py
@@ -11,6 +11,7 @@
 STATE = 16
 RANK = 128
 GROUP = 8
+STREAMS = 4
 VMEM_LIMIT = 48 * 1024 * 1024
 
 
@@ -110,7 +111,7 @@
     ring_send, ring_recv, x_send, x_recv, c_send, c_recv, local_sem,
 ):
     rows = normed_ref.shape[0]
-    half = rows // 2
+    piece = rows // STREAMS
     depth = win_ref.shape[1]
     req, seq = lax.axis_index("req"), lax.axis_index("seq")
     place = ring_place(seq, n)
@@ -146,19 +147,22 @@
         copy.start()
 
     ring = []
+    latest = [None] * STREAMS
     for step in range(n - 1):
-        pair = []
-        for way in range(2):
-            part = pl.ds(way * half, half)
-            turn = place + (n - step if way == 0 else step)
+        for way in range(STREAMS):
+            part = pl.ds(way * piece, piece)
+            turn = place + (n - step if way % 2 == 0 else step)
             owner = ring_index(turn % n, n)
             src = normed_ref.at[part] if step == 0 else act_ref.at[owner, part]
             copy = remote(
                 src, act_ref.at[owner, part], ring_send.at[way, step], ring_recv.at[way, step],
-                right if way == 0 else left,
+                right if way % 2 == 0 else left,
             )
+            if step > 0:
+                latest[way].wait_recv()
             copy.start()
-            pair.append(copy)
+            latest[way] = copy
+            ring.append(copy)
         if step == n - 2:
             for hop in range(1, chips):
                 owner = ((chip + chips - hop) % chips) * 2 + core
@@ -173,9 +177,8 @@
                     if hop < chips - 1:
                         crossing.append(remote(block, block, x_send.at[which, hop], x_recv.at[which, hop], ahead))
                         crossing[-1].start()
-        for copy in pair:
-            copy.wait_recv()
-        ring += pair
+    for copy in latest:
+        copy.wait_recv()
     for copy in ring:
         copy.wait_send()
     for copy in pending:
@@ -199,7 +202,7 @@
         in_specs=[anywhere] * 3,
         out_specs=(anywhere,) * 3,
         scratch_shapes=[
-            dma((2, n - 1)), dma((2, n - 1)), dma((2, m // 2 - 1)), dma((2, m // 2 - 1)),
+            dma((STREAMS, n - 1)), dma((STREAMS, n - 1)), dma((2, m // 2 - 1)), dma((2, m // 2 - 1)),
             dma((2, m // 2)), dma((2, m // 2)), dma((3,)),
         ],
         compiler_params=pltpu.CompilerParams(
@@ -209,7 +212,9 @@
     )(normed, win, wout)
 
 
-def total_kernel(n, inner_ref, weight_ref, sum_ref, send_buf, recv_buf, own_buf, send, recv, send2, recv2):
+def total_kernel(
+    n, inner_ref, weight_ref, act_ref, gate_ref, sum_ref, zgate_ref, send_buf, recv_buf, own_buf, send, recv, send2, recv2,
+):
     req, seq = lax.axis_index("req"), lax.axis_index("seq")
     rows = inner_ref.shape[0] // n
     peers = [(req, (seq + d) % n) for d in range(1, n)]
@@ -219,6 +224,14 @@
         return lax.dot_general(
             weight_ref[...], block, (((1,), (1,)), ((), ())), preferred_element_type=jnp.float32
         )
+
+    def gates(first_block, last_block):
+        @pl.loop(first_block, last_block)
+        def _(i):
+            here = pl.ds(pl.multiple_of(i * rows, rows), rows)
+            zgate_ref[here, :] = jnp.dot(
+                act_ref[here, :], gate_ref[...], preferred_element_type=jnp.float32
+            ).astype(jnp.bfloat16)
 
     greet(peers)
     first = []
@@ -228,6 +241,7 @@
         copy.start()
         first.append(copy)
     total = partial(seq)
+    gates(0, n // 2)
     for d in range(1, n):
         first[d - 1].wait_recv()
         total = total + recv_buf[d - 1].astype(jnp.float32)
@@ -238,21 +252,25 @@
         copy.start()
         second.append(copy)
     sum_ref[seq] = own_buf[...]
+    gates(n // 2, n)
     for copy in second:
         copy.wait()
     for copy in first:
         copy.wait_send()
 
 
-def total_call(n, inner, weight):
+def total_call(n, inner, weight, act, gate):
     vmem = pl.BlockSpec(memory_space=pltpu.VMEM)
     dma = pltpu.SemaphoreType.DMA
     columns, rows = weight.shape[0], inner.shape[0] // n
     return pl.pallas_call(
         functools.partial(total_kernel, n),
-        out_shape=jax.ShapeDtypeStruct((n, columns, rows), jnp.bfloat16),
-        in_specs=[vmem, vmem],
-        out_specs=vmem,
+        out_shape=(
+            jax.ShapeDtypeStruct((n, columns, rows), jnp.bfloat16),
+            jax.ShapeDtypeStruct(inner.shape, jnp.bfloat16),
+        ),
+        in_specs=[vmem] * 4,
+        out_specs=(vmem, vmem),
         scratch_shapes=[
             pltpu.VMEM((n - 1, columns, rows), jnp.bfloat16),
             pltpu.VMEM((n - 1, columns, rows), jnp.bfloat16),
@@ -262,7 +280,7 @@
             collective_id=1, has_side_effects=True, vmem_limit_bytes=VMEM_LIMIT
         ),
         name="total",
-    )(inner, weight)
+    )(inner, weight, act, gate)
 
 
 def output_kernel(
@@ -270,7 +288,7 @@
     send_buf, recv_buf, acc_ref, send, recv, state_send, state_recv,
 ):
     rows, model = hidden_ref.shape
-    half = model // 2
+    part = model // STREAMS
     req, seq = lax.axis_index("req"), lax.axis_index("seq")
     place = ring_place(seq, n)
     right = (req, ring_index((place + 1) % n, n))
@@ -287,41 +305,41 @@
     def hop(way, step):
         return remote(
             send_buf.at[way, step], recv_buf.at[way, step], send.at[way, step], recv.at[way, step],
-            right if way == 0 else left,
+            right if way % 2 == 0 else left,
         )
 
     def product(way, step):
-        turn = place + (2 * n - 1 - step if way == 0 else 1 + step)
+        turn = place + (2 * n - 1 - step if way % 2 == 0 else 1 + step)
         owner = ring_index(turn % n, n)
         block = gated_ref[pl.ds(pl.multiple_of(owner * rows, rows), rows), :]
         acc_ref[way] = jnp.dot(
-            block, wout_ref[:, way * half : (way + 1) * half], preferred_element_type=jnp.float32
+            block, wout_ref[:, way * part : (way + 1) * part], preferred_element_type=jnp.float32
         )
 
-    for way in range(2):
+    for way in range(STREAMS):
         product(way, 0)
         send_buf[way, 0] = acc_ref[way].astype(jnp.bfloat16)
         hop(way, 0).start()
 
     def middle(step, carry):
-        for way in range(2):
+        for way in range(STREAMS):
             product(way, step)
-        for way in range(2):
+        for way in range(STREAMS):
             hop(way, step - 1).wait_recv()
             send_buf[way, step] = (acc_ref[way] + recv_buf[way, step - 1].astype(jnp.float32)).astype(jnp.bfloat16)
             hop(way, step).start()
         return carry
 
     lax.fori_loop(1, n - 1, middle, 0)
-    for way in range(2):
+    for way in range(STREAMS):
         product(way, n - 1)
-    for way in range(2):
+    for way in range(STREAMS):
         hop(way, n - 2).wait_recv()
-        columns = slice(way * half, (way + 1) * half)
+        columns = slice(way * part, (way + 1) * part)
         branch = acc_ref[way] + recv_buf[way, n - 2].astype(jnp.float32)
         mixed_ref[:, columns] = (hidden_ref[:, columns].astype(jnp.float32) + branch).astype(jnp.bfloat16)
     for step in range(n - 1):
-        for way in range(2):
+        for way in range(STREAMS):
             hop(way, step).wait_send()
     for copy in states:
         copy.wait()
@@ -340,10 +358,10 @@
         in_specs=[vmem] * 4,
         out_specs=(vmem, vmem),
         scratch_shapes=[
-            pltpu.VMEM((2, n - 1, rows, model // 2), jnp.bfloat16),
-            pltpu.VMEM((2, n - 1, rows, model // 2), jnp.bfloat16),
-            pltpu.VMEM((2, rows, model // 2), jnp.float32),
-            dma((2, n - 1)), dma((2, n - 1)), dma((m - 1,)), dma((m - 1,)),
+            pltpu.VMEM((STREAMS, n - 1, rows, model // STREAMS), jnp.bfloat16),
+            pltpu.VMEM((STREAMS, n - 1, rows, model // STREAMS), jnp.bfloat16),
+            pltpu.VMEM((STREAMS, rows, model // STREAMS), jnp.float32),
+            dma((STREAMS, n - 1)), dma((STREAMS, n - 1)), dma((m - 1,)), dma((m - 1,)),
         ],
         compiler_params=pltpu.CompilerParams(
             collective_id=2, has_side_effects=True, vmem_limit_bytes=VMEM_LIMIT
@@ -381,14 +399,13 @@
     act, w_in, w_out = gather_call(seq_count, req_count, normed, in_weight, out_weight)
     act = act.reshape(span, -1)
     xin = jnp.dot(act, w_in[0], preferred_element_type=jnp.float32)
-    zgate = jnp.dot(act, w_in[1], preferred_element_type=jnp.float32).astype(jnp.bfloat16)
     padded = jnp.pad(xin, ((taps_count - 1, 0), (0, 0)))
     taps = conv_weight.astype(jnp.float32)
     convolved = conv_bias.astype(jnp.float32) + jnp.zeros_like(xin)
     for tap in range(taps_count):
         convolved = convolved + taps[tap] * padded[tap : tap + span, :]
     inner = jax.nn.silu(convolved).astype(jnp.bfloat16)
-    sums = total_call(seq_count, inner, xproj_weight.T)
+    sums, zgate = total_call(seq_count, inner, xproj_weight.T, act, w_in[1])
     length_here = lax.dynamic_slice_in_dim(lengths, req_index, 1, 0)
     alog = lax.dynamic_slice_in_dim(a_log, seq_index * width, width, 1)
     skip = lax.dynamic_slice_in_dim(skip_gain, seq_index * width, width, 0)[None]

time: 162 us -> 147 us (0.907)
  Pallas kernels: 140 us -> 127 us
  matrix products: 10.4 us -> 5.34 us
  local copies, waits for them, and re-layouts: 3.97 us -> 8.03 us
    pallas_call x1, Pallas kernels: 53.9 us -> 44.2 us  [output_call(): pl.pallas_call(functools.partial(output_kernel, n, m), out_shape=(jax.Sha...]
    pallas_call x1, Pallas kernels: 52.2 us -> 46.2 us  [gather_call(): pl.pallas_call(functools.partial(gather_kernel, n, m), out_shape=(jax.Sha...]
    dot_general x1 -> x0, matrix products: 5.22 us -> none  [per_device(): jnp.dot(act, w_in[1], preferred_element_type=jnp.float32)]
    unnamed x27 -> x33, local copies, waits for them, and re-layouts: 2.61 us -> 6.53 us
    pallas_call x1, Pallas kernels: 17.5 us -> 20.4 us  [total_call(): pl.pallas_call(functools.partial(total_kernel, n), out_shape=(jax.ShapeDt...]
where the time goes in v4:
time: 147 us
  Pallas kernels  127 us (86%)
  local copies, waits for them, and re-layouts  8.03 us (5%)
  matrix products  5.34 us (4%)
  other arithmetic  5.3 us (4%)
    pallas_call x1, Pallas kernels, gather_call(): pl.pallas_call(functools.partial(gather_kernel, n, m), out_shape=(jax.Sha...  46.2 us
    pallas_call x1, Pallas kernels, output_call(): pl.pallas_call(functools.partial(output_kernel, n, m), out_shape=(jax.Sha...  44.2 us
    pallas_call x1, Pallas kernels, total_call(): pl.pallas_call(functools.partial(total_kernel, n), out_shape=(jax.ShapeDt...  20.4 us
    pallas_call x1, Pallas kernels, scan_call(): pl.pallas_call(scan_kernel, out_shape=(jax.ShapeDtypeStruct((span, width)...  16.4 us
    unnamed x33, local copies, waits for them, and re-layouts  6.53 us
    dot_general x1, matrix products, per_device(): xin = jnp.dot(act, w_in[0], preferred_element_type=jnp.float32)  5.34 us

profile of v4, /device:TPU:0, one launch (start us, length us, event | category | flops | bytes accessed | tf_op | source)
XLA Modules:
  0.0 146.7 jit_solution(4638616629934699195)
XLA Ops:
  0.6 0.0 copy-start
  0.6 0.0 copy-start.2
  0.7 0.8 convert_element_type.26
  1.4 1.2 fusion.5
  2.7 1.2 fusion.7.normed_ref
  3.9 0.0 copy-done.2
  3.9 0.0 copy-start.3
  3.9 1.0 copy-done.3
  5.0 46.2 %gather.1 = (bf16[8,128,2048]{2,1,0:T(8,128)(2,1)}, bf16[2,2048,512]{2,1,0:T(8,128)(2,1)}, bf16[512,2048]{1,0:T(8,128)(2,1)S(1)}) custom-call(bf16[128,2048]{1,0:T(8,128)(2,1)S(1)} %fusion.7.normed_ref, bf16[2,512,512]{2,1,0:T(8,128)(2,1)S(1)} %copy-done.2, bf16[512,512]{1,0:T(8,128)(2,1)S(1)} %copy-done.3), custom_call_target="tpu_custom_call" | custom-call | tf_op jit(solution)/shard_map/gather/pallas_call | solution.py:195
  51.2 0.0 copy-start.11
  51.2 0.0 copy-start.12
  51.2 0.0 copy-start.10
  51.2 5.3 %fusion = f32[1024,512]{1,0:T(8,128)S(1)} fusion(bf16[1024,2048]{1,0:T(8,128)(2,1)} %bitcast.22, bf16[2,2048,512]{2,1,0:T(8,128)(2,1)} %get-tuple-element.12), kind=kOutput, calls=%fused_computation | convolution fusion | flops 2147483648 | bytes 8388608 | tf_op jit(solution)/shard_map/dot_general | solution.py:401
  56.6 0.0 copy-done.11
  56.6 0.0 copy-done.12
  56.6 1.3 multiply_convert_fusion.inner_ref
  58.0 0.0 copy-done.10
  58.0 0.0 copy-start.4
  58.0 0.1 slice_bitcast_fusion.gate_ref
  58.1 0.8 copy-done.4
  58.9 0.0 copy-start.14
  58.9 0.0 copy-start.13
  58.9 0.0 copy-start.9
  58.9 20.4 %total.1 = (bf16[8,160,128]{2,1,0:T(8,128)(2,1)S(1)}, bf16[1024,512]{1,0:T(8,128)(2,1)S(1)}) custom-call(bf16[1024,512]{1,0:T(8,128)(2,1)S(1)} %multiply_convert_fusion.inner_ref, bf16[160,512]{1,0:T(8,128)(2,1)S(1)} %bitcast.20, bf16[1024,2048]{1,0:T(8,128)(2,1)} %bitcast.23, bf16[2048,512]{1,0:T(8,128)(2,1)S(1)} %slice_bitcast_fusion.gate_ref), custom_call_target="tpu_custom_call" | custom-call | tf_op jit(solution)/shard_map/total/pallas_call | solution.py:266
  79.3 0.0 copy-start.5
  79.3 1.0 copy-done.5
  80.3 0.0 copy-start.7
  80.3 0.7 copy-done.7
  81.0 0.0 copy-done.14
  81.0 0.6 dynamic_slice.9.length_ref
  81.6 0.0 copy-done
  81.6 0.8 dynamic_slice.11
  82.4 0.0 copy-done.13
  82.4 0.0 copy-done.9
  82.4 0.0 copy-start.6
  82.4 1.2 copy-done.6
  83.6 0.0 copy-start.8
  83.6 1.0 copy-done.8
  84.6 0.0 copy-start.1
  84.6 16.4 %scan.1 = (bf16[1024,512]{1,0:T(8,128)(2,1)S(1)}, f32[16,512]{1,0:T(8,128)S(1)}) custom-call(s32[1]{0:T(128)} %dynamic_slice.9.length_ref, bf16[8,160,128]{2,1,0:T(8,128)(2,1)S(1)} %copy-done.8, bf16[1024,512]{1,0:T(8,128)(2,1)S(1)} %multiply_convert_fusion.inner_ref, bf16[1024,512]{1,0:T(8,128)(2,1)S(1)} %copy-done.6, bf16[128,512]{1,0:T(8,128)(2,1)S(1)} %copy-done.9, ...), custom_call_target="tpu_custom_call" | custom-call | flops 58720256 | bytes 4194304 | tf_op jit(solution)/shard_map/scan/pallas_call | solution.py:66
  101.0 0.0 copy-start.15
  101.0 0.0 copy-done.1
  101.0 44.2 %output.1 = (bf16[128,2048]{1,0:T(8,128)(2,1)S(1)}, f32[4,16,512]{2,1,0:T(8,128)S(1)}) custom-call(bf16[1024,512]{1,0:T(8,128)(2,1)S(1)} %get-tuple-element.15.gated_ref, bf16[512,2048]{1,0:T(8,128)(2,1)S(1)} %get-tuple-element.16.wout_ref, bf16[128,2048]{1,0:T(8,128)(2,1)S(1)} %bitcast.18, f32[16,512]{1,0:T(8,128)S(1)} %get-tuple-element.17.state_ref), custom_call_target="tpu_custom_call" | custom-call | tf_op jit(solution)/shard_map/output/pallas_call | solution.py:352
  145.2 0.0 copy-done.15
  145.2 0.7 multiply_reduce_fusion
  145.9 0.8 copy.16
  (6 shorter events, 0.0 us)
Async XLA Ops:
  0.6 81.0 %copy-start = (f32[16,4096]{1,0:T(8,128)S(1)}, f32[16,4096]{1,0:T(8,128)}, u32[]{:S(2)}) copy-start(f32[16,4096]{1,0:T(8,128)} %param.23) | copy-start | bytes 786436
  0.6 3.3 %copy-start.2 = (bf16[2,512,512]{2,1,0:T(8,128)(2,1)S(1)}, bf16[2,512,512]{2,1,0:T(8,128)(2,1)}, u32[]{:S(2)}) copy-start(bf16[2,512,512]{2,1,0:T(8,128)(2,1)} %win_ref.1) | copy-start | bytes 3145732
  3.9 1.0 copy-start.3
  51.2 5.4 %copy-start.11 = (bf16[4,512]{1,0:T(4,128)(2,1)S(1)}, bf16[4,512]{1,0:T(4,128)(2,1)}, u32[]{:S(2)}) copy-start(bf16[4,512]{1,0:T(4,128)(2,1)} %param.18) | copy-start | bytes 12292
  51.2 5.4 %copy-start.12 = (bf16[512]{0:T(512)(128)(2,1)S(1)}, bf16[512]{0:T(512)(128)(2,1)}, u32[]{:S(2)}) copy-start(bf16[512]{0:T(512)(128)(2,1)} %param.19) | copy-start | bytes 3076
  51.2 6.7 %copy-start.10 = (bf16[2,2048,512]{2,1,0:T(8,128)(2,1)S(1)}, bf16[2,2048,512]{2,1,0:T(8,128)(2,1)}, u32[]{:S(2)}) copy-start(bf16[2,2048,512]{2,1,0:T(8,128)(2,1)} %get-tuple-element.12) | copy-start | bytes 12582916
  58.0 0.9 copy-start.4
  58.9 22.1 %copy-start.14 = (s32[4]{0:T(128)S(1)}, s32[4]{0:T(128)}, u32[]{:S(2)}) copy-start(s32[4]{0:T(128)} %param.14) | copy-start | bytes 52
  58.9 23.5 %copy-start.13 = (bf16[512]{0:T(512)(128)(2,1)S(1)}, bf16[512]{0:T(512)(128)(2,1)}, u32[]{:S(2)}) copy-start(bf16[512]{0:T(512)(128)(2,1)} %param.22) | copy-start | bytes 3076
  58.9 23.5 %copy-start.9 = (bf16[128,512]{1,0:T(8,128)(2,1)S(1)}, bf16[128,512]{1,0:T(8,128)(2,1)}, u32[]{:S(2)}) copy-start(bf16[128,512]{1,0:T(8,128)(2,1)} %dtw_ref.1) | copy-start | bytes 393220
  79.3 1.0 copy-start.5
  80.3 0.7 copy-start.7
  82.4 1.2 copy-start.6
  83.6 1.0 copy-start.8
  84.6 16.4 %copy-start.1 = (bf16[1,128,2048]{2,1,0:T(8,128)(2,1)S(1)}, bf16[1,128,2048]{2,1,0:T(8,128)(2,1)}, u32[]{:S(2)}) copy-start(bf16[1,128,2048]{2,1,0:T(8,128)(2,1)} %param.13) | copy-start | bytes 1572868
  101.0 44.2 %copy-start.15 = (s32[4]{0:T(128)S(1)}, s32[4]{0:T(128)}, u32[]{:S(2)}) copy-start(s32[4]{0:T(128)} %param.15) | copy-start | bytes 52
